TPU v7x, 256 devices: a whole 4x4x8 slice. The times are simulated.
256 devices in a mesh: board: 32 (over y_hi, z, core), hist: 4 (over x), pair: 2 (over y_lo).
Axes of the slice: x: 4, y: 4 (y_hi: 2, y_lo: 2; y = y_hi * 2 + y_lo), z: 8, core: 2. Of those that a mesh axis runs over, the one named last changes fastest.
Arguments:
- turn_reach: bfloat16 [2, 2048, 4, 256], P('pair', 'board', None, 'hist'), may hold values from 0.0099487305 to 1
- regrets: float32 [2, 32, 256, 2048], P('pair', 'board', 'hist'), may hold values from -6 to 6
- pot: float32 [256], P('hist'), may hold values from 0.5 to 4
- turn_cluster: int32 [32], P('board'), may hold values from 0 to 3
- bucket_map: int32 [32, 2048], P('board'), may hold values from 0 to 2047
- codes: int32 [256], P('hist'), may hold values from 0 to 2, as said below
- ranks: int32 [32, 2048], P('board'), may hold values from 0 to 2047
Outputs:
- new_regrets: float32 [2, 32, 256, 2048], P('pair', 'board', 'hist')
- turn_values: float32 [2, 2048, 4, 256], P('pair', 'board', None, 'hist')
Inputs may be any that keep to these rules, and one draw needn't show every extreme that they name: `codes`: 0: player 0 folded, 1: player 1 folded, 2: showdown; a function of the history alone: among the 4 siblings of each node exactly one is a fold (0 or 1), the others are 2. Equal ranks tie.
All inputs are finite; a program needn't handle non-finite values.
Results may differ from a plain program's by a relative error of at most 0.0018.
Values may be sent and summed in bfloat16 or wider, within the bound.
A program may use at most 64 MiB of HBM per device.

v0:
```python
import jax
import jax.numpy as jnp
from jax import lax
from jax.sharding import PartitionSpec as P

KR = 2048
KT = 2048
H = 256
ACTIONS = 4


SMOOTH = 0.01


def from_partner(array, axis, distance):
    return lax.ppermute(array, axis, [(i, i ^ 1 << distance) for i in range(lax.axis_size(axis))])


def on_device(turn_reach, regrets, pot, turn_cluster, bucket_map, codes, ranks):
    player = lax.axis_index("pair")
    scale = KR ** (-0.5)
    regret_now = regrets[0]
    boards, rows_here, width = regret_now.shape
    nodes = H // ACTIONS
    local_actions = rows_here // nodes
    grouped = regret_now.reshape(boards, local_actions, nodes, width)
    positive = jnp.maximum(grouped, 0.0)
    sibling_total = lax.psum(jnp.sum(positive, axis=1), "hist")
    sigma = ((positive + SMOOTH) / (sibling_total[:, None] + ACTIONS * SMOOTH)).reshape(
        boards, rows_here, width
    )
    clusters = turn_reach.shape[2]
    cluster_hot = (turn_cluster[:, None] == jnp.arange(clusters, dtype=jnp.int32)[None, :]).astype(
        jnp.bfloat16
    )
    piece = lax.all_gather(turn_reach, "board", axis=1, tiled=True)
    count = piece.shape[1]
    chosen = jnp.einsum(
        "bt,cth->bhc", cluster_hot, piece[0], preferred_element_type=jnp.float32
    ).astype(jnp.bfloat16)
    columns = jnp.arange(count, dtype=jnp.int32)

    def lift_per_board(items):
        panel, mapping = items
        onehot = (mapping[:, None] == columns[None, :]).astype(jnp.bfloat16)
        return jnp.einsum("hc,kc->hk", panel, onehot, preferred_element_type=jnp.float32)

    lifted = lax.map(lift_per_board, (chosen, bucket_map))
    reach = (lifted * sigma).astype(jnp.bfloat16)

    def equity(items):
        panel, rank = items
        block = min(512, width)
        result = jnp.zeros((rows_here, width), jnp.float32)
        for first in range(0, width, block):
            strength = jnp.sign(rank[:, None] - rank[None, first : first + block]).astype(
                jnp.bfloat16
            )
            result = result + jnp.einsum(
                "hj,kj->hk",
                panel[:, first : first + block],
                strength,
                preferred_element_type=jnp.float32,
            )
        return result

    opposite = from_partner(reach, "pair", 0)
    opp_show = lax.map(equity, (opposite, ranks))
    opp_total = jnp.sum(opposite.astype(jnp.float32), axis=2)
    signs = jnp.where(codes == player, -1.0, 1.0).astype(jnp.float32)
    fold = (signs[None, :] * pot[None, :] * scale * opp_total)[:, :, None]
    show = pot[None, :, None] * scale * opp_show
    value = jnp.where((codes == 2)[None, :, None], show, fold)
    weighted = sigma * value
    node = lax.psum(jnp.sum(weighted.reshape(boards, local_actions, nodes, width), axis=1), "hist")
    updated = (
        grouped + value.reshape(boards, local_actions, nodes, width) - node[:, None]
    ).reshape(boards, rows_here, width)
    carried = weighted.astype(jnp.bfloat16)
    cluster_mask = cluster_hot.astype(jnp.float32)
    project_columns = jnp.arange(KT, dtype=jnp.int32)

    def project_per_board(running, items):
        panel, mapping, mask = items
        onehot = (mapping[:, None] == project_columns[None, :]).astype(jnp.bfloat16)
        part = jnp.einsum("kc,hk->ch", onehot, panel, preferred_element_type=jnp.float32)
        return (running + part[:, None, :] * mask[None, :, None], None)

    running, unused = lax.scan(
        project_per_board,
        jnp.zeros((KT, clusters, rows_here), jnp.float32),
        (carried, bucket_map, cluster_mask),
    )
    shares = lax.psum_scatter(running, "board", scatter_dimension=0, tiled=True)
    return (updated[None], shares[None])


def solution(mesh):
    return jax.shard_map(
        on_device,
        mesh=mesh,
        in_specs=(
            P("pair", "board", None, "hist"),
            P("pair", "board", "hist", None),
            P("hist"),
            P("board"),
            P("board", None),
            P("hist"),
            P("board", None),
        ),
        out_specs=(P("pair", "board", "hist", None), P("pair", "board", None, "hist")),
        check_vma=False,
    )
```

profile of v0, /device:TPU:1, one launch (start us, length us, event | category | flops | bytes accessed | tf_op | source)
XLA Modules:
  0.0 461.3 jit_solution(12884510239772482737)
XLA Ops:
  8.0 0.0 all-gather.2.cloned.1.call-start
  8.1 0.7 all-gather.2.cloned.1.call-update
  8.8 0.0 all-reduce.5.cloned.1.call-start
  8.8 1.9 maximum_bitcast_fusion
  10.7 0.0 all-reduce.5.cloned.1.call-update
  10.7 0.0 all-reduce.7.cloned.1.call-start
  11.4 0.7 broadcast_compare_fusion
  12.1 83.8 %all-gather.2.cloned.1.call-done = bf16[1,2048,4,64]{3,2,0,1:T(4,128)(2,1)} async-done(((bf16[1,64,4,64]{3,2,0,1:T(4,128)(2,1)}), bf16[1,2048,4,64]{3,2,0,1:T(4,128)(2,1)}) %all-gather.2.cloned.1.call-update) | async-done | bytes 1048592 | tf_op jit(solution)/shard_map/all_gather | solution.py:36
  95.9 12.2 %multiply_reduce_fusion = bf16[2048,64]{1,0:T(8,128)(2,1)S(1)} fusion(f32[4]{0:T(128)S(1)} %bitcast_convert_fusion, bf16[1,2048,4,64]{3,2,0,1:T(4,128)(2,1)} %all-gather.2.cloned.1.call-done), kind=kLoop, calls=%fused_computation.6 | loop fusion | flops 1441792 | bytes 1310736 | tf_op jit(solution)/shard_map/bt,cth->bhc/dot_general | solution.py:38
  108.1 0.0 all-reduce.5.cloned.1.call-done
  108.2 0.0 copy-start.2
  108.2 4.7 %fusion.12 = bf16[1,64,2048]{2,1,0:T(8,128)(2,1)S(1)} fusion(s32[2048]{0:T(1024)S(1)} %bitcast.67, bf16[2048,64]{1,0:T(8,128)(2,1)S(1)} %multiply_reduce_fusion, f32[1,64,2048]{2,1,0:T(8,128)} %all-reduce.5.cloned.1.call-done, f32[1,1,64,2048]{3,2,1,0:T(8,128)S(1)} %copy-done), kind=kOutput, calls=%fused_computation.18 | convolution fusion | flops 541851648 | bytes 1581056 | tf_op jit(solution)/shard_map/while/body/eval_jaxpr/hc,kc->hk/dot_general | solution.py:46
  112.9 0.0 copy-start.3
  112.9 0.4 collective-permute-start
  113.3 7.3 %collective-permute-done = bf16[1,64,2048]{2,1,0:T(8,128)(2,1)S(1)} collective-permute-done((bf16[1,64,2048]{2,1,0:T(8,128)(2,1)S(1)}, bf16[1,64,2048]{2,1,0:T(8,128)(2,1)S(1)}, u32[]{:S(2)}, u32[]{:S(2)}) %collective-permute-start) | collective-permute-done | bytes 262176 | tf_op jit(solution)/shard_map/ppermute | solution.py:16
  120.7 1.2 fusion.15
  121.8 1.2 fusion.14
  123.0 1.2 fusion.13
  124.2 0.1 convert_reduce_fusion
  124.3 1.3 fusion.9
  125.6 0.9 fusion.28
  126.6 0.0 all-reduce.7.cloned.1.call-update
  126.6 0.2 all-reduce.9.cloned.1.call-start
  126.8 2.9 fusion.2
  129.7 0.0 copy-start.6
  129.7 2.4 broadcast_multiply_fusion
  132.1 0.0 all-reduce.9.cloned.1.call-update
  132.1 0.6 dynamic-slice
  133.4 36.0 %all-reduce.7.cloned.1.call-done = f32[1,1,64,2048]{3,2,1,0:T(8,128)} async-done(((f32[1,1,64,2048]{3,2,1,0:T(8,128)}), f32[1,1,64,2048]{3,2,1,0:T(8,128)}) %all-reduce.7.cloned.1.call-update) | async-done | bytes 524304 | tf_op jit(solution)/shard_map/psum | solution.py:75
  169.4 1.9 fusion.25
  171.3 280.8 %all-reduce.9.cloned.1.call-done = f32[2048,4,64]{2,1,0:T(4,128)} async-done(((f32[2048,4,64]{2,1,0:T(4,128)}), f32[2048,4,64]{2,1,0:T(4,128)}) %all-reduce.9.cloned.1.call-update) | async-done | bytes 2097168
  452.1 1.6 dynamic-slice_bitcast_fusion
  (15 shorter events, 0.0 us)
Async XLA Ops:
  8.0 100.2 %copy-start = (f32[1,1,64,2048]{3,2,1,0:T(8,128)S(1)}, f32[1,1,64,2048]{3,2,1,0:T(8,128)}, u32[]{:S(2)}) copy-start(f32[1,1,64,2048]{3,2,1,0:T(8,128)} %param.8) | copy-start | bytes 1572868
  8.0 100.2 %copy-start.5 = (s32[1,2048]{1,0:T(1,128)S(1)}, s32[1,2048]{1,0:T(1,128)}, u32[]{:S(2)}) copy-start(s32[1,2048]{1,0:T(1,128)} %param.11) | copy-start | bytes 24580
  8.0 87.9 %all-gather.2.cloned.1.call-start = ((), (), s32[]{:S(2)}) async-start(), calls=%async_computation | async-start | bytes 2162688 | tf_op jit(solution)/shard_map/all_gather | solution.py:36
  8.8 99.4 %all-reduce.5.cloned.1.call-start = ((), (), s32[]{:S(2)}) async-start(), calls=%async_computation.1 | async-start | bytes 1048576 | tf_op jit(solution)/shard_map/psum | solution.py:28
  10.7 158.7 %all-reduce.7.cloned.1.call-start = ((), (), s32[]{:S(2)}) async-start(), calls=%async_computation.2 | async-start | bytes 1048576 | tf_op jit(solution)/shard_map/psum | solution.py:75
  108.2 5.1 %copy-start.2 = (s32[1,2048]{1,0:T(1,128)S(1)}, s32[1,2048]{1,0:T(1,128)}, u32[]{:S(2)}) copy-start(s32[1,2048]{1,0:T(1,128)} %param.13) | copy-start | bytes 24580
  112.9 11.4 %copy-start.3 = (f32[64]{0:T(128)S(1)}, f32[64]{0:T(128)}, u32[]{:S(2)}) copy-start(f32[64]{0:T(128)} %param.9) | copy-start | bytes 772
  112.9 11.4 %copy-start.4 = (s32[64]{0:T(128)S(1)}, s32[64]{0:T(128)}, u32[]{:S(2)}) copy-start(s32[64]{0:T(128)} %param.12) | copy-start | bytes 772
  112.9 7.7 %collective-permute-start = (bf16[1,64,2048]{2,1,0:T(8,128)(2,1)S(1)}, bf16[1,64,2048]{2,1,0:T(8,128)(2,1)S(1)}, u32[]{:S(2)}, u32[]{:S(2)}) collective-permute-start(bf16[1,64,2048]{2,1,0:T(8,128)(2,1)S(1)} %fusion.12), channel_id=1, source_target_pairs={{0,1},{1,0},{2,3},{3,2},{4,5},{5,4},{6,7},{7,6},{8,9},{9,8},{10,11... | collective-permute-start | bytes 786440 | tf_op jit(solution)/shard_map/ppermute | solution.py:16
  121.8 3.8 copy-start.1
  126.6 325.6 %all-reduce.9.cloned.1.call-start = ((), (), s32[]{:S(2)}) async-start(), calls=%async_computation.3 | async-start | bytes 8388608
  129.7 2.5 copy-start.6
Sparse Core Ops, SparseCore 0:
  11.6 84.2 all-gather.1
Sparse Core Ops, SparseCore 1:
  12.1 49.6 all-reduce.4
  126.7 42.7 all-reduce.6
  171.9 280.1 all-reduce.8
where the time goes:
time: 462 us; the launch traced here: 461 us
  waiting for transfers between devices  409 us (89%)
  other arithmetic  20.2 us (4%)
  between operations  17.1 us (4%)
  matrix products  12.3 us (3%)
    unnamed x5, waiting for transfers between devices  282 us
    all_gather x1, waiting for transfers between devices, on_device(): piece = lax.all_gather(turn_reach, 'board', axis=1, tiled=True)  83.8 us
    psum x1, waiting for transfers between devices, on_device(): lax.psum(jnp.sum(weighted.reshape(boards, local_actions, nodes, width), a...  36 us
    dot_general x1, other arithmetic, on_device(): jnp.einsum('bt,cth->bhc', cluster_hot, piece[0], preferred_element_type=j...  12.2 us
  transfers between devices with their start and end apart: 5, of which 4 were waited for; matrix products, arithmetic and copies ran while one was open for 5% of the time, Pallas kernels for 0%

commit v1 on v0

v1 whole, which is shorter than its diff:
```python
import functools

import jax
import jax.numpy as jnp
from jax import lax
from jax.experimental import pallas as pl
from jax.experimental.pallas import tpu as pltpu
from jax.sharding import PartitionSpec as P

ACTIONS = 4
CLUSTERS = 4
PLAYERS = 2
SMOOTH = 0.01
CHUNK = 8
SLOTS = PLAYERS * ACTIONS
ROWS = SLOTS * CHUNK
HALVES = 2
PIECE = 64
LANES = 128
MESH = pl.DeviceIdType.MESH


def kernel(
    ring,
    regrets,
    turn,
    pot,
    codes,
    cluster,
    mapping,
    ranks,
    fresh,
    shares,
    onehot,
    strength,
    meta_out,
    meta,
    regret,
    sigma,
    near,
    cluster_out,
    clusters,
    far_out,
    far,
    reach,
    updated,
    weighted,
    back_out,
    back,
    last_out,
    last,
    regret_send,
    regret_recv,
    meta_send,
    meta_recv,
    near_send,
    near_recv,
    cluster_send,
    cluster_recv,
    far_send,
    far_recv,
    fresh_send,
    fresh_recv,
    back_send,
    back_recv,
    last_send,
    last_recv,
    local_sem,
):
    width = ranks.shape[1]
    depth = ring * LANES
    board = lax.axis_index("board")
    action = lax.axis_index("hist")
    player = lax.axis_index("pair")
    half = board // ring
    place = board % ring
    chunk = action * PLAYERS + player
    slot = player * ACTIONS + action
    group = half * SLOTS + chunk
    scale = width ** (-0.5)

    def same_board(step):
        other = (chunk + step) % SLOTS
        return other, {"board": board, "hist": other // PLAYERS, "pair": other % PLAYERS}

    def near_peer(step):
        other = (group + step) % (HALVES * SLOTS)
        their_chunk = other % SLOTS
        target = {
            "board": (other // SLOTS) * ring + place,
            "hist": their_chunk // PLAYERS,
            "pair": their_chunk % PLAYERS,
        }
        return other, target

    def far_peer(step):
        other = (place + step) % ring
        return other, {"board": half * ring + other, "hist": action, "pair": player}

    def regret_copy(step):
        other, target = same_board(step)
        return pltpu.make_async_remote_copy(
            src_ref=regrets.at[pl.ds(pl.multiple_of(other * CHUNK, CHUNK), CHUNK)],
            dst_ref=regret.at[slot],
            send_sem=regret_send.at[step],
            recv_sem=regret_recv.at[step],
            device_id=target,
            device_id_type=MESH,
        )

    def meta_copy(step):
        other, target = same_board(step)
        return pltpu.make_async_remote_copy(
            src_ref=meta_out.at[other],
            dst_ref=meta.at[slot],
            send_sem=meta_send.at[step],
            recv_sem=meta_recv.at[step],
            device_id=target,
            device_id_type=MESH,
        )

    def near_copy(step):
        other, target = near_peer(step)
        return pltpu.make_async_remote_copy(
            src_ref=turn.at[other % SLOTS],
            dst_ref=near.at[half * SLOTS + slot],
            send_sem=near_send.at[step],
            recv_sem=near_recv.at[step],
            device_id=target,
            device_id_type=MESH,
        )

    def cluster_copy(step):
        other, target = far_peer(step)
        return pltpu.make_async_remote_copy(
            src_ref=cluster_out,
            dst_ref=clusters.at[place],
            send_sem=cluster_send.at[step],
            recv_sem=cluster_recv.at[step],
            device_id=target,
            device_id_type=MESH,
        )

    def far_copy(step):
        other, target = far_peer(step)
        return pltpu.make_async_remote_copy(
            src_ref=far_out.at[other],
            dst_ref=far.at[:, pl.ds(pl.multiple_of(place * LANES, LANES), LANES)],
            send_sem=far_send.at[step],
            recv_sem=far_recv.at[step],
            device_id=target,
            device_id_type=MESH,
        )

    def fresh_copy(step):
        other, target = same_board(step)
        their_slot = (other % PLAYERS) * ACTIONS + other // PLAYERS
        return pltpu.make_async_remote_copy(
            src_ref=updated.at[their_slot],
            dst_ref=fresh.at[pl.ds(pl.multiple_of(chunk * CHUNK, CHUNK), CHUNK)],
            send_sem=fresh_send.at[step],
            recv_sem=fresh_recv.at[step],
            device_id=target,
            device_id_type=MESH,
        )

    def back_copy(step):
        other, target = far_peer(step)
        return pltpu.make_async_remote_copy(
            src_ref=back_out.at[other],
            dst_ref=back.at[place],
            send_sem=back_send.at[step],
            recv_sem=back_recv.at[step],
            device_id=target,
            device_id_type=MESH,
        )

    def last_copy(step):
        other, target = near_peer(step)
        their_chunk = other % SLOTS
        their_slot = (their_chunk % PLAYERS) * ACTIONS + their_chunk // PLAYERS
        return pltpu.make_async_remote_copy(
            src_ref=last_out.at[(other // SLOTS) * SLOTS + their_slot],
            dst_ref=last.at[half * SLOTS + chunk],
            send_sem=last_send.at[step],
            recv_sem=last_recv.at[step],
            device_id=target,
            device_id_type=MESH,
        )

    def each(count, action_of):
        def body(step, carry):
            action_of(step)
            return carry

        lax.fori_loop(1, count, body, 0)

    barrier = pltpu.get_barrier_semaphore()

    def greet_near(step):
        other, target = near_peer(step)
        pl.semaphore_signal(barrier, inc=1, device_id=target, device_id_type=MESH)

    def greet_far(step):
        other, target = far_peer(step)
        pl.semaphore_signal(barrier, inc=1, device_id=target, device_id_type=MESH)

    each(HALVES * SLOTS, greet_near)
    each(ring, greet_far)

    own_cluster = jnp.full((1, LANES), cluster[0], jnp.int32)
    cluster_out[...] = own_cluster
    clusters[place] = own_cluster
    nodes = SLOTS * CHUNK
    line = lax.broadcasted_iota(jnp.int32, (nodes, nodes), 0)
    column = lax.broadcasted_iota(jnp.int32, (nodes, nodes), 1)
    diagonal = line == column
    pot_rows = jnp.sum(jnp.where(diagonal, pot[...], 0.0), axis=1, keepdims=True)
    code_rows = jnp.sum(
        jnp.where(diagonal, codes[...].astype(jnp.float32), 0.0), axis=1, keepdims=True
    )
    meta_out[:, :, :LANES] = jnp.broadcast_to(pot_rows, (nodes, LANES)).reshape(
        SLOTS, CHUNK, LANES
    )
    meta_out[:, :, LANES:] = jnp.broadcast_to(code_rows, (nodes, LANES)).reshape(
        SLOTS, CHUNK, LANES
    )
    pl.semaphore_wait(barrier, HALVES * SLOTS - 1 + ring - 1)

    each(HALVES * SLOTS, lambda step: near_copy(step).start())
    each(ring, lambda step: cluster_copy(step).start())
    each(SLOTS, lambda step: regret_copy(step).start())
    each(SLOTS, lambda step: meta_copy(step).start())
    keep_regret = pltpu.make_async_copy(
        regrets.at[pl.ds(pl.multiple_of(chunk * CHUNK, CHUNK), CHUNK)],
        regret.at[slot],
        local_sem.at[0],
    )
    keep_regret.start()
    near[half * SLOTS + slot] = turn[chunk]
    meta[slot] = meta_out[chunk]

    rank_row = ranks[...].astype(jnp.float32)

    def build_strength(block, carry):
        first = pl.multiple_of(block * LANES, LANES)
        mine = ranks[:, pl.ds(first, LANES)].astype(jnp.float32)
        rank_column = jnp.broadcast_to(mine, (LANES, LANES)).T
        for tile in range(width // LANES):
            span = slice(tile * LANES, (tile + 1) * LANES)
            sign = jnp.minimum(jnp.maximum(rank_row[:, span] - rank_column, -1.0), 1.0)
            strength[pl.ds(first, LANES), span] = sign.astype(jnp.bfloat16)
        return carry

    lax.fori_loop(0, width // LANES, build_strength, 0)

    each(HALVES * SLOTS, lambda step: near_copy(step).wait_recv())
    each(ring, lambda step: cluster_copy(step).wait_recv())
    low = lax.broadcasted_iota(jnp.int32, (SLOTS, CHUNK, LANES), 2) < PIECE
    parts = []
    lower = near[:SLOTS].astype(jnp.float32)
    upper = near[SLOTS:].astype(jnp.float32)
    for pair in range(CLUSTERS // 2):
        rows = slice(pair * CHUNK, (pair + 1) * CHUNK)
        first, second = lower[:, rows], upper[:, rows]
        parts.append(jnp.where(low, first, pltpu.roll(second, PIECE, 2)))
        parts.append(jnp.where(low, pltpu.roll(first, PIECE, 2), second))
    panels = [part.reshape(ROWS, LANES) for part in parts]

    def choose(step, carry):
        other = (place + step) % ring
        wanted = clusters[other]
        result = panels[0]
        for index in range(1, CLUSTERS):
            result = jnp.where(wanted == index, panels[index], result)
        far_out[other] = result.astype(jnp.bfloat16)
        return carry

    def choose_and_send(step):
        choose(step, 0)
        far_copy(step).start()

    each(ring, choose_and_send)
    choose(0, 0)
    far[:, pl.ds(pl.multiple_of(place * LANES, LANES), LANES)] = far_out[place]

    bucket = mapping[...]
    shard, within = bucket // PIECE, bucket % PIECE
    ordered = (shard % ring) * LANES + (shard // ring) * PIECE + within

    def build_onehot(block, carry):
        first = pl.multiple_of(block * LANES, LANES)
        index = lax.broadcasted_iota(jnp.int32, (LANES, LANES), 0) + first
        for tile in range(width // LANES):
            span = slice(tile * LANES, (tile + 1) * LANES)
            hit = jnp.where(ordered[:, span] == index, 1.0, 0.0)
            onehot[pl.ds(first, LANES), span] = hit.astype(jnp.bfloat16)
        return carry

    lax.fori_loop(0, depth // LANES, build_onehot, 0)

    each(SLOTS, lambda step: regret_copy(step).wait_recv())
    keep_regret.wait()
    each(SLOTS, lambda step: meta_copy(step).wait_recv())
    step_width = min(256, width)

    def match(tile, carry):
        span = pl.ds(pl.multiple_of(tile * step_width, step_width), step_width)
        for who in range(PLAYERS):
            positive = [
                jnp.maximum(regret[who * ACTIONS + act, :, span], 0.0) for act in range(ACTIONS)
            ]
            total = (positive[0] + positive[1]) + (positive[2] + positive[3])
            inverse = 1.0 / (total + ACTIONS * SMOOTH)
            for act in range(ACTIONS):
                sigma[who * ACTIONS + act, :, span] = (positive[act] + SMOOTH) * inverse
        return carry

    lax.fori_loop(0, width // step_width, match, 0)

    each(ring, lambda step: far_copy(step).wait_recv())

    def lift(tile, totals):
        span = pl.ds(pl.multiple_of(tile * step_width, step_width), step_width)
        lifted = jnp.dot(far[...], onehot[:, span], preferred_element_type=jnp.float32)
        now = (lifted * sigma[:, :, span].reshape(ROWS, step_width)).astype(jnp.bfloat16)
        reach[:, span] = now
        return totals + jnp.sum(now.astype(jnp.float32), axis=1, keepdims=True)

    totals = lax.fori_loop(0, width // step_width, lift, jnp.zeros((ROWS, 1), jnp.float32))

    def opponent(rows):
        return jnp.concatenate([rows[ROWS // 2 :], rows[: ROWS // 2]], axis=0)

    pot_here = meta[:, :, :LANES].reshape(ROWS, LANES) * scale
    code_here = meta[:, :, LANES:].reshape(ROWS, LANES)
    row = lax.broadcasted_iota(jnp.int32, (ROWS, LANES), 0)
    who_here = jnp.where(row >= ROWS // 2, 1.0, 0.0)
    signed = jnp.where(code_here == who_here, -pot_here, pot_here)
    fold = signed * opponent(totals)
    repeats = step_width // LANES
    fold_wide = jnp.concatenate([fold] * repeats, axis=1)
    pot_wide = jnp.concatenate([pot_here] * repeats, axis=1)
    show_wide = jnp.concatenate([code_here] * repeats, axis=1) == 2.0

    def evaluate(tile, carry):
        span = pl.ds(pl.multiple_of(tile * step_width, step_width), step_width)
        equity = jnp.dot(reach[...], strength[:, span], preferred_element_type=jnp.float32)
        value = jnp.where(show_wide, pot_wide * opponent(equity), fold_wide)
        value = value.reshape(PLAYERS, ACTIONS, CHUNK, step_width)
        play = sigma[:, :, span].reshape(PLAYERS, ACTIONS, CHUNK, step_width)
        share = play * value
        node = (share[:, 0] + share[:, 1]) + (share[:, 2] + share[:, 3])
        before = regret[:, :, span].reshape(PLAYERS, ACTIONS, CHUNK, step_width)
        after = (before + value) - node[:, None]
        updated[:, :, span] = after.reshape(SLOTS, CHUNK, step_width)
        weighted[:, span] = share.reshape(ROWS, step_width).astype(jnp.bfloat16)
        return carry

    lax.fori_loop(0, width // step_width, evaluate, 0)

    each(SLOTS, lambda step: fresh_copy(step).start())
    keep_fresh = pltpu.make_async_copy(
        updated.at[slot],
        fresh.at[pl.ds(pl.multiple_of(chunk * CHUNK, CHUNK), CHUNK)],
        local_sem.at[1],
    )
    keep_fresh.start()

    def project(step):
        other = (place + step) % ring
        rows = pl.ds(pl.multiple_of(other * LANES, LANES), LANES)
        block = lax.dot_general(
            weighted[...],
            onehot[rows, :],
            (((1,), (1,)), ((), ())),
            preferred_element_type=jnp.float32,
        )
        back_out[other] = block.astype(jnp.bfloat16)

    def project_and_send(step):
        project(step)
        back_copy(step).start()

    each(ring, project_and_send)
    project(0)
    back[place] = back_out[place]

    each(ring, lambda step: back_copy(step).wait_recv())
    held = [jnp.zeros((ROWS, LANES), jnp.float32) for unused in range(CLUSTERS)]
    for source in range(ring):
        block = back[source].astype(jnp.float32)
        theirs = clusters[source]
        for index in range(CLUSTERS):
            held[index] = held[index] + jnp.where(theirs == index, block, 0.0)
    held = [part.reshape(SLOTS, CHUNK, LANES) for part in held]
    for pair in range(CLUSTERS // 2):
        rows = slice(pair * CHUNK, (pair + 1) * CHUNK)
        first, second = held[2 * pair], held[2 * pair + 1]
        last_out[:SLOTS, rows] = jnp.where(low, first, pltpu.roll(second, PIECE, 2))
        last_out[SLOTS:, rows] = jnp.where(low, pltpu.roll(first, PIECE, 2), second)

    each(HALVES * SLOTS, lambda step: last_copy(step).start())
    last[half * SLOTS + chunk] = last_out[half * SLOTS + slot]
    each(HALVES * SLOTS, lambda step: last_copy(step).wait_recv())
    shares[...] = last[:SLOTS] + last[SLOTS:]

    each(SLOTS, lambda step: fresh_copy(step).wait_recv())
    keep_fresh.wait()

    def finish_same(step):
        regret_copy(step).wait_send()
        meta_copy(step).wait_send()
        fresh_copy(step).wait_send()

    def finish_near(step):
        near_copy(step).wait_send()
        last_copy(step).wait_send()

    def finish_far(step):
        cluster_copy(step).wait_send()
        far_copy(step).wait_send()
        back_copy(step).wait_send()

    each(SLOTS, finish_same)
    each(HALVES * SLOTS, finish_near)
    each(ring, finish_far)


def on_device(ring, turn_reach, regrets, pot, turn_cluster, bucket_map, codes, ranks):
    width = ranks.shape[1]
    depth = ring * LANES
    near = HALVES * SLOTS
    halves = CLUSTERS // 2
    tile = (halves * CHUNK, 2 * PIECE)
    turn = (
        turn_reach[0]
        .reshape(PIECE, halves, 2, SLOTS, CHUNK)
        .transpose(3, 1, 4, 2, 0)
        .reshape(SLOTS, *tile)
    )
    vmem = pl.BlockSpec(memory_space=pltpu.VMEM)
    dma = pltpu.SemaphoreType.DMA
    fresh, shares = pl.pallas_call(
        functools.partial(kernel, ring),
        out_shape=(
            jax.ShapeDtypeStruct((SLOTS * CHUNK, width), jnp.float32),
            jax.ShapeDtypeStruct((SLOTS, *tile), jnp.float32),
        ),
        in_specs=[
            pl.BlockSpec(memory_space=pl.ANY),
            vmem,
            vmem,
            vmem,
            pl.BlockSpec(memory_space=pltpu.SMEM),
            vmem,
            vmem,
        ],
        out_specs=(pl.BlockSpec(memory_space=pl.ANY), vmem),
        scratch_shapes=[
            pltpu.VMEM((depth, width), jnp.bfloat16),
            pltpu.VMEM((width, width), jnp.bfloat16),
            pltpu.VMEM((SLOTS, CHUNK, 2 * LANES), jnp.float32),
            pltpu.VMEM((SLOTS, CHUNK, 2 * LANES), jnp.float32),
            pltpu.VMEM((SLOTS, CHUNK, width), jnp.float32),
            pltpu.VMEM((SLOTS, CHUNK, width), jnp.float32),
            pltpu.VMEM((near, *tile), jnp.bfloat16),
            pltpu.VMEM((1, LANES), jnp.int32),
            pltpu.VMEM((ring, 1, LANES), jnp.int32),
            pltpu.VMEM((ring, ROWS, LANES), jnp.bfloat16),
            pltpu.VMEM((ROWS, depth), jnp.bfloat16),
            pltpu.VMEM((ROWS, width), jnp.bfloat16),
            pltpu.VMEM((SLOTS, CHUNK, width), jnp.float32),
            pltpu.VMEM((ROWS, width), jnp.bfloat16),
            pltpu.VMEM((ring, ROWS, LANES), jnp.bfloat16),
            pltpu.VMEM((ring, ROWS, LANES), jnp.bfloat16),
            pltpu.VMEM((near, *tile), jnp.float32),
            pltpu.VMEM((near, *tile), jnp.float32),
            dma((SLOTS,)),
            dma((SLOTS,)),
            dma((SLOTS,)),
            dma((SLOTS,)),
            dma((near,)),
            dma((near,)),
            dma((ring,)),
            dma((ring,)),
            dma((ring,)),
            dma((ring,)),
            dma((SLOTS,)),
            dma((SLOTS,)),
            dma((ring,)),
            dma((ring,)),
            dma((near,)),
            dma((near,)),
            dma((2,)),
        ],
        compiler_params=pltpu.CompilerParams(
            collective_id=0, has_side_effects=True, vmem_limit_bytes=40 * 2**20
        ),
    )(
        regrets[0, 0],
        turn,
        pot[None],
        codes[None],
        turn_cluster,
        bucket_map,
        ranks,
    )
    shares = (
        shares.reshape(SLOTS, halves, CHUNK, 2, PIECE)
        .transpose(4, 1, 3, 0, 2)
        .reshape(1, PIECE, CLUSTERS, SLOTS * CHUNK)
    )
    return fresh[None, None], shares


def solution(mesh):
    return jax.shard_map(
        functools.partial(on_device, mesh.shape["board"] // HALVES),
        mesh=mesh,
        in_specs=(
            P("pair", "board", None, "hist"),
            P("pair", "board", "hist", None),
            P("hist"),
            P("board"),
            P("board", None),
            P("hist"),
            P("board", None),
        ),
        out_specs=(P("pair", "board", "hist", None), P("pair", "board", None, "hist")),
        check_vma=False,
    )
```

time: 462 us -> 53.4 us (0.12)
  waiting for transfers between devices: 409 us -> 0 us
  Pallas kernels: 0 us -> 47.4 us
  other arithmetic: 20.2 us -> 0 us
  between operations: 17.1 us -> 1.35 us
  matrix products: 12.3 us -> 0 us
    unnamed x5 -> x0, waiting for transfers between devices: 282 us -> none
    all_gather x1 -> x0, waiting for transfers between devices: 83.8 us -> none  [on_device(): piece = lax.all_gather(turn_reach, 'board', axis=1, tiled=True)]
    pallas_call x0 -> x1, Pallas kernels: none -> 47.4 us  [on_device(): pl.pallas_call(functools.partial(kernel, ring), out_shape=(jax.ShapeDtype...]
    psum x2 -> x0, waiting for transfers between devices: 36.1 us -> none  [the longest x1 36 us: on_device(): lax.psum(jnp.sum(weighted.reshape(boards, local_actions, nodes, width), a...]
    dot_general x6 -> x0, matrix products: 12.3 us -> none  [the longest x4 4.77 us: equity(): jnp.einsum('hj,kj->hk', panel[:, first:first + block], strength, preferre...]
    dot_general x1 -> x0, other arithmetic: 12.2 us -> none  [on_device(): jnp.einsum('bt,cth->bhc', cluster_hot, piece[0], preferred_element_type=j...]
    ppermute x1 -> x0, waiting for transfers between devices: 7.33 us -> none  [from_partner(): lax.ppermute(array, axis, [(i, i ^ 1 << distance) for i in range(lax.axis...]
  transfers between devices with their start and end apart: 5 -> 0, of which waited for: 4 -> 0; matrix products, arithmetic and copies ran while one was open for 5% -> 0% of each run, Pallas kernels for 0% -> 0%
where the time goes in v1:
time: 53.4 us; the launch traced here: 53.1 us
  Pallas kernels  47.4 us (89%)
  local copies, waits for them, and re-layouts  4.43 us (8%)
  between operations  1.35 us (3%)
    pallas_call x1, Pallas kernels, on_device(): pl.pallas_call(functools.partial(kernel, ring), out_shape=(jax.ShapeDtype...  47.4 us
    unnamed x13, local copies, waits for them, and re-layouts  4.12 us

profile of v1, /device:TPU:1, one launch (start us, length us, event | category | flops | bytes accessed | tf_op | source)
XLA Modules:
  0.0 53.1 jit_solution(111989049684066943)
XLA Ops:
  1.3 0.9 %copy.11 = bf16[1,64,4,64]{1,3,2,0:T(8,128)(2,1)S(1)} copy(bf16[1,64,4,64]{3,2,1,0:T(4,128)(2,1)} %param.7) | data formatting | bytes 65536 | tf_op args[0]
  2.2 0.1 copy.12
  2.3 0.0 copy-start.1
  2.3 0.0 copy-start.2
  2.3 0.0 copy-start.3
  2.3 0.0 copy-start.4
  2.3 0.1 reshape.13.turn
  2.4 0.6 %copy-done.1 = s32[1,2048]{1,0:T(1,128)S(1)} copy-done((s32[1,2048]{1,0:T(1,128)S(1)}, s32[1,2048]{1,0:T(1,128)}, u32[]{:S(2)}) %copy-start.1) | copy-done | bytes 8216
  3.0 0.0 copy-done.2
  3.0 0.0 copy-done.3
  3.0 0.0 copy-done.4
  3.0 0.0 copy-start
  3.0 1.0 %copy-done = f32[1,1,64,2048]{3,2,1,0:T(8,128)S(1)} copy-done((f32[1,1,64,2048]{3,2,1,0:T(8,128)S(1)}, f32[1,1,64,2048]{3,2,1,0:T(8,128)}, u32[]{:S(2)}) %copy-start) | copy-done | bytes 524312
  4.1 47.4 %shard_map.86 = (f32[64,2048]{1,0:T(8,128)S(1)}, f32[8,16,128]{2,1,0:T(8,128)S(1)}) custom-call(f32[64,2048]{1,0:T(8,128)S(1)} %bitcast.10, bf16[8,16,128]{2,1,0:T(8,128)(2,1)S(1)} %reshape.13.turn, f32[1,64]{1,0:T(1,128)S(1)} %bitcast.12, s32[1,64]{1,0:T(1,128)S(1)} %bitcast.13, s32[1]{0:T(128)S(6)} %copy.16.cluster, s32[1,2048]{1,0:T(1,128)S(1)} %copy-done.1, ...), custom_call_target="tpu_custom_call" | custom-call | tf_op jit(solution)/shard_map/pallas_call | solution.py:444
  51.4 0.1 reshape.14
  51.6 0.8 %copy.14 = f32[1,64,4,64]{3,2,1,0:T(4,128)} copy(f32[1,64,4,64]{1,3,2,0:T(8,128)S(1)} %bitcast.14) | data formatting | bytes 131072
  52.3 0.8 %copy.17 = f32[1,1,64,2048]{3,2,1,0:T(8,128)} copy(f32[1,1,64,2048]{3,2,1,0:T(8,128)S(1)} %bitcast.11) | data formatting | bytes 1048576
  (1 shorter events, 0.0 us)
Async XLA Ops:
  2.3 0.7 %copy-start.1 = (s32[1,2048]{1,0:T(1,128)S(1)}, s32[1,2048]{1,0:T(1,128)}, u32[]{:S(2)}) copy-start(s32[1,2048]{1,0:T(1,128)} %mapping.1) | copy-start | bytes 24580
  2.3 0.7 %copy-start.2 = (s32[1,2048]{1,0:T(1,128)S(1)}, s32[1,2048]{1,0:T(1,128)}, u32[]{:S(2)}) copy-start(s32[1,2048]{1,0:T(1,128)} %ranks.1) | copy-start | bytes 24580
  2.3 0.7 %copy-start.3 = (f32[64]{0:T(128)S(1)}, f32[64]{0:T(128)}, u32[]{:S(2)}) copy-start(f32[64]{0:T(128)} %param.9) | copy-start | bytes 772
  2.3 0.7 %copy-start.4 = (s32[64]{0:T(128)S(1)}, s32[64]{0:T(128)}, u32[]{:S(2)}) copy-start(s32[64]{0:T(128)} %param.12) | copy-start | bytes 772
  3.0 1.0 %copy-start = (f32[1,1,64,2048]{3,2,1,0:T(8,128)S(1)}, f32[1,1,64,2048]{3,2,1,0:T(8,128)}, u32[]{:S(2)}) copy-start(f32[1,1,64,2048]{3,2,1,0:T(8,128)} %param.8) | copy-start | bytes 1572868

commit v2 on v1

v2 whole, which is shorter than its diff:
```python
import functools

import jax
import jax.numpy as jnp
from jax import lax
from jax.experimental import pallas as pl
from jax.experimental.pallas import tpu as pltpu
from jax.sharding import PartitionSpec as P

ACTIONS = 4
CLUSTERS = 4
PLAYERS = 2
SMOOTH = 0.01
CHUNK = 8
SLOTS = PLAYERS * ACTIONS
ROWS = SLOTS * CHUNK
HALVES = 2
PIECE = 64
CORES = 2
LANES = 128
MESH = pl.DeviceIdType.MESH


def kernel(
    regrets,
    turn_reach,
    pot,
    codes,
    cluster,
    mapping,
    ranks,
    fresh,
    shares,
    onehot,
    spread,
    strength,
    turn_raw,
    turn_rows,
    turn,
    pot_row,
    code_row,
    map_row,
    rank_row,
    meta_out,
    meta,
    regret,
    sigma,
    near,
    cluster_out,
    clusters,
    far_out,
    far,
    lifted,
    reach,
    updated,
    weighted,
    back_out,
    back,
    last_out,
    last,
    fetch_sem,
    regret_send,
    regret_recv,
    meta_send,
    meta_recv,
    near_send,
    near_recv,
    cluster_send,
    cluster_recv,
    far_send,
    far_recv,
    fresh_send,
    fresh_recv,
    back_send,
    back_recv,
    last_send,
    last_recv,
    local_sem,
):
    width = ranks.shape[1]
    ring = far_send.shape[0]
    chips = ring // CORES
    board = lax.axis_index("board")
    action = lax.axis_index("hist")
    player = lax.axis_index("pair")
    half = board // ring
    place = board % ring
    chip = place // CORES
    core = place % CORES
    chunk = action * PLAYERS + player
    slot = player * ACTIONS + action
    group = half * SLOTS + chunk
    scale = width ** (-0.5)
    inward = [(i + 1) // 2 if i % 2 else (chips - i // 2) % chips for i in range(chips)]
    outward = inward[::-1]

    def same_board(step):
        other = (chunk + step) % SLOTS
        return other, {"board": board, "hist": other // PLAYERS, "pair": other % PLAYERS}

    def near_peer(step):
        other = (group + step) % (HALVES * SLOTS)
        their_chunk = other % SLOTS
        target = {
            "board": (other // SLOTS) * ring + place,
            "hist": their_chunk // PLAYERS,
            "pair": their_chunk % PLAYERS,
        }
        return other, target

    def far_peer(step):
        there = (chip + step // CORES) % chips
        mate = (core + step) % CORES
        other = there * CORES + mate
        target = {"board": half * ring + other, "hist": action, "pair": player}
        return there, mate, other, target

    def lanes_of(index):
        return pl.ds(pl.multiple_of(index * LANES, LANES), LANES)

    def chunk_of(index):
        return pl.ds(pl.multiple_of(index * CHUNK, CHUNK), CHUNK)

    def remote(src, dst, send, recv, step, target):
        return pltpu.make_async_remote_copy(
            src_ref=src,
            dst_ref=dst,
            send_sem=send.at[step],
            recv_sem=recv.at[step],
            device_id=target,
            device_id_type=MESH,
        )

    def regret_copy(step):
        other, target = same_board(step)
        return remote(
            regrets.at[chunk_of(other)], regret.at[slot], regret_send, regret_recv, step, target
        )

    def meta_copy(step):
        other, target = same_board(step)
        return remote(meta_out.at[other], meta.at[slot], meta_send, meta_recv, step, target)

    def near_copy(step):
        other, target = near_peer(step)
        return remote(
            turn.at[other % SLOTS],
            near.at[half * SLOTS + slot],
            near_send,
            near_recv,
            step,
            target,
        )

    def cluster_copy(step):
        there, mate, other, target = far_peer(step)
        return remote(cluster_out, clusters.at[place], cluster_send, cluster_recv, step, target)

    def far_copy(step):
        there, mate, other, target = far_peer(step)
        return remote(
            far_out.at[other], far.at[chip, :, lanes_of(core)], far_send, far_recv, step, target
        )

    def fresh_copy(step):
        other, target = same_board(step)
        their_slot = (other % PLAYERS) * ACTIONS + other // PLAYERS
        return remote(
            updated.at[their_slot],
            fresh.at[chunk_of(chunk)],
            fresh_send,
            fresh_recv,
            step,
            target,
        )

    def back_copy(step):
        there, mate, other, target = far_peer(step)
        return remote(
            back_out.at[there, :, lanes_of(mate)],
            back.at[place],
            back_send,
            back_recv,
            step,
            target,
        )

    def last_copy(step):
        other, target = near_peer(step)
        their_chunk = other % SLOTS
        their_slot = (their_chunk % PLAYERS) * ACTIONS + their_chunk // PLAYERS
        return remote(
            last_out.at[(other // SLOTS) * SLOTS + their_slot],
            last.at[half * SLOTS + chunk],
            last_send,
            last_recv,
            step,
            target,
        )

    def each(count, action_of):
        def body(step, carry):
            action_of(step)
            return carry

        lax.fori_loop(1, count, body, 0)

    fetches = [
        pltpu.make_async_copy(src, dst, fetch_sem.at[index])
        for index, (src, dst) in enumerate(
            [
                (turn_reach, turn_raw),
                (pot, pot_row),
                (codes, code_row),
                (ranks, rank_row),
                (mapping, map_row),
                (regrets.at[chunk_of(chunk)], regret.at[slot]),
            ]
        )
    ]
    for fetch in fetches:
        fetch.start()

    barrier = pltpu.get_barrier_semaphore()

    def greet_near(step):
        other, target = near_peer(step)
        pl.semaphore_signal(barrier, inc=1, device_id=target, device_id_type=MESH)

    def greet_far(step):
        there, mate, other, target = far_peer(step)
        pl.semaphore_signal(barrier, inc=1, device_id=target, device_id_type=MESH)

    each(ring, greet_far)
    each(HALVES * SLOTS, greet_near)

    own_cluster = jnp.full((1, LANES), cluster[0], jnp.int32)
    cluster_out[...] = own_cluster
    clusters[place] = own_cluster
    for fetch in fetches[:3]:
        fetch.wait()
    nodes = SLOTS * CHUNK
    turn_rows[...] = turn_raw[...].astype(jnp.float32)
    columns = []
    for pair in range(CLUSTERS // 2):
        both = jnp.concatenate([turn_rows[:, 2 * pair, :], turn_rows[:, 2 * pair + 1, :]], axis=0)
        columns.append(both.T.reshape(SLOTS, CHUNK, 2 * PIECE))
    turn[...] = jnp.concatenate(columns, axis=1).astype(jnp.bfloat16)
    line = lax.broadcasted_iota(jnp.int32, (nodes, nodes), 0)
    column = lax.broadcasted_iota(jnp.int32, (nodes, nodes), 1)
    diagonal = line == column
    pot_rows = jnp.sum(jnp.where(diagonal, pot_row[...], 0.0), axis=1, keepdims=True)
    code_rows = jnp.sum(
        jnp.where(diagonal, code_row[...].astype(jnp.float32), 0.0), axis=1, keepdims=True
    )
    meta_out[:, :, :LANES] = jnp.broadcast_to(pot_rows, (nodes, LANES)).reshape(
        SLOTS, CHUNK, LANES
    )
    meta_out[:, :, LANES:] = jnp.broadcast_to(code_rows, (nodes, LANES)).reshape(
        SLOTS, CHUNK, LANES
    )
    near[half * SLOTS + slot] = turn[chunk]
    meta[slot] = meta_out[chunk]
    pl.semaphore_wait(barrier, HALVES * SLOTS - 1 + ring - 1)

    each(HALVES * SLOTS, lambda step: near_copy(step).start())
    each(ring, lambda step: cluster_copy(step).start())
    each(SLOTS, lambda step: meta_copy(step).start())
    each(SLOTS, lambda step: regret_copy(step).start())

    for fetch in fetches[3:5]:
        fetch.wait()
    rank_wide = rank_row[...].astype(jnp.float32)

    def build_strength(block, carry):
        mine = rank_row[:, lanes_of(block)].astype(jnp.float32)
        rank_column = jnp.broadcast_to(mine, (LANES, LANES)).T
        for tile in range(width // LANES):
            span = slice(tile * LANES, (tile + 1) * LANES)
            sign = jnp.minimum(jnp.maximum(rank_wide[:, span] - rank_column, -1.0), 1.0)
            strength[lanes_of(block), span] = sign.astype(jnp.bfloat16)
        return carry

    lax.fori_loop(0, width // LANES, build_strength, 0)

    each(HALVES * SLOTS, lambda step: near_copy(step).wait_recv())
    each(ring, lambda step: cluster_copy(step).wait_recv())
    low = lax.broadcasted_iota(jnp.int32, (SLOTS, CHUNK, LANES), 2) < PIECE
    parts = []
    lower = near[:SLOTS].astype(jnp.float32)
    upper = near[SLOTS:].astype(jnp.float32)
    for pair in range(CLUSTERS // 2):
        rows = slice(pair * CHUNK, (pair + 1) * CHUNK)
        first, second = lower[:, rows], upper[:, rows]
        parts.append(jnp.where(low, first, pltpu.roll(second, PIECE, 2)))
        parts.append(jnp.where(low, pltpu.roll(first, PIECE, 2), second))
    panels = [part.reshape(ROWS, LANES) for part in parts]

    def choose(other):
        wanted = clusters[other]
        result = panels[0]
        for index in range(1, CLUSTERS):
            result = jnp.where(wanted == index, panels[index], result)
        return result.astype(jnp.bfloat16)

    for distance in outward:
        for step in range(distance * CORES, (distance + 1) * CORES):
            if step > 0:
                there, mate, other, target = far_peer(step)
                far_out[other] = choose(other)
                far_copy(step).start()
    far[chip, :, lanes_of(core)] = choose(place)

    bucket = map_row[...]
    shard, within = bucket // PIECE, bucket % PIECE
    map_row[...] = (shard % ring) * LANES + (shard // ring) * PIECE + within
    map_wide = map_row[...]
    tiles = ring * LANES // LANES

    def build_onehot(block, carry):
        index = lax.broadcasted_iota(jnp.int32, (LANES, LANES), 0) + block * LANES
        for tile in range(width // LANES):
            span = slice(tile * LANES, (tile + 1) * LANES)
            hit = jnp.where(map_wide[:, span] == index, 1.0, 0.0)
            onehot[lanes_of(block), span] = hit.astype(jnp.bfloat16)
        return carry

    lax.fori_loop(0, tiles, build_onehot, 0)

    def build_spread(block, carry):
        mine = map_row[:, lanes_of(block)].astype(jnp.float32)
        map_column = jnp.broadcast_to(mine, (LANES, LANES)).T.astype(jnp.int32)
        index = lax.broadcasted_iota(jnp.int32, (LANES, LANES), 1)
        for tile in range(tiles):
            span = slice(tile * LANES, (tile + 1) * LANES)
            hit = jnp.where(map_column == index + tile * LANES, 1.0, 0.0)
            spread[lanes_of(block), span] = hit.astype(jnp.bfloat16)
        return carry

    lax.fori_loop(0, width // LANES, build_spread, 0)

    step_width = min(512, width)
    spans = [slice(first, first + step_width) for first in range(0, width, step_width)]

    def match(span):
        for who in range(PLAYERS):
            positive = [
                jnp.maximum(regret[who * ACTIONS + act, :, span], 0.0) for act in range(ACTIONS)
            ]
            total = (positive[0] + positive[1]) + (positive[2] + positive[3])
            inverse = 1.0 / (total + ACTIONS * SMOOTH)
            for act in range(ACTIONS):
                sigma[who * ACTIONS + act, :, span] = (positive[act] + SMOOTH) * inverse

    totals = jnp.zeros((ROWS, 1), jnp.float32)
    for turn_of, distance in enumerate(inward):
        if turn_of == chips // 2:
            each(SLOTS, lambda step: regret_copy(step).wait_recv())
            fetches[5].wait()
            for span in spans:
                match(span)
        for step in range(distance * CORES, (distance + 1) * CORES):
            if step > 0:
                far_copy(step).wait_recv()
        source = (chip + chips - distance) % chips
        rows = pl.ds(pl.multiple_of(source * CORES * LANES, CORES * LANES), CORES * LANES)
        panel = far[source]
        for span in spans:
            now = jnp.dot(panel, onehot[rows, span], preferred_element_type=jnp.float32)
            if turn_of > 0:
                now = now + lifted[:, span]
            if turn_of < chips - 1:
                lifted[:, span] = now
            else:
                now = (now * sigma[:, :, span].reshape(ROWS, step_width)).astype(jnp.bfloat16)
                reach[:, span] = now
                totals = totals + jnp.sum(now.astype(jnp.float32), axis=1, keepdims=True)

    def opponent(rows):
        return jnp.concatenate([rows[ROWS // 2 :], rows[: ROWS // 2]], axis=0)

    each(SLOTS, lambda step: meta_copy(step).wait_recv())
    pot_here = meta[:, :, :LANES].reshape(ROWS, LANES) * scale
    code_here = meta[:, :, LANES:].reshape(ROWS, LANES)
    row = lax.broadcasted_iota(jnp.int32, (ROWS, LANES), 0)
    who_here = jnp.where(row >= ROWS // 2, 1.0, 0.0)
    signed = jnp.where(code_here == who_here, -pot_here, pot_here)
    fold = signed * opponent(totals)
    repeats = step_width // LANES
    fold_wide = jnp.concatenate([fold] * repeats, axis=1)
    pot_wide = jnp.concatenate([pot_here] * repeats, axis=1)
    show_wide = jnp.concatenate([code_here] * repeats, axis=1) == 2.0

    for span in spans:
        equity = jnp.dot(reach[...], strength[:, span], preferred_element_type=jnp.float32)
        value = jnp.where(show_wide, pot_wide * opponent(equity), fold_wide)
        updated[:, :, span] = value.reshape(SLOTS, CHUNK, step_width)
        share = sigma[:, :, span].reshape(ROWS, step_width) * value
        weighted[:, span] = share.astype(jnp.bfloat16)

    for distance in outward:
        there = (chip + distance) % chips
        columns_there = pl.ds(pl.multiple_of(there * CORES * LANES, CORES * LANES), CORES * LANES)
        block = jnp.dot(
            weighted[...], spread[:, columns_there], preferred_element_type=jnp.float32
        )
        back_out[there] = block.astype(jnp.bfloat16)
        for step in range(distance * CORES, (distance + 1) * CORES):
            if step > 0:
                back_copy(step).start()
    back[place] = back_out[chip, :, lanes_of(core)]

    def renew(tile, carry):
        span = lanes_of(tile)
        for who in range(PLAYERS):
            those = [who * ACTIONS + act for act in range(ACTIONS)]
            value = [updated[index, :, span] for index in those]
            share = [sigma[index, :, span] * now for index, now in zip(those, value)]
            node = (share[0] + share[1]) + (share[2] + share[3])
            for index, now in zip(those, value):
                updated[index, :, span] = (regret[index, :, span] + now) - node
        return carry

    lax.fori_loop(0, width // LANES, renew, 0)
    each(SLOTS, lambda step: fresh_copy(step).start())
    keep_fresh = pltpu.make_async_copy(updated.at[slot], fresh.at[chunk_of(chunk)], local_sem)
    keep_fresh.start()

    held = [jnp.zeros((ROWS, LANES), jnp.float32) for unused in range(CLUSTERS)]
    for distance in inward:
        for step in range(distance * CORES, (distance + 1) * CORES):
            if step > 0:
                back_copy(step).wait_recv()
            source = ((chip + chips - distance) % chips) * CORES + (core + step) % CORES
            block = back[source].astype(jnp.float32)
            theirs = clusters[source]
            for index in range(CLUSTERS):
                held[index] = held[index] + jnp.where(theirs == index, block, 0.0)
    held = [part.reshape(SLOTS, CHUNK, LANES) for part in held]
    for pair in range(CLUSTERS // 2):
        rows = slice(pair * CHUNK, (pair + 1) * CHUNK)
        first, second = held[2 * pair], held[2 * pair + 1]
        last_out[:SLOTS, rows] = jnp.where(low, first, pltpu.roll(second, PIECE, 2))
        last_out[SLOTS:, rows] = jnp.where(low, pltpu.roll(first, PIECE, 2), second)

    each(HALVES * SLOTS, lambda step: last_copy(step).start())
    last[half * SLOTS + chunk] = last_out[half * SLOTS + slot]

    def finish_far(step):
        cluster_copy(step).wait_send()
        far_copy(step).wait_send()
        back_copy(step).wait_send()

    def finish_same(step):
        regret_copy(step).wait_send()
        meta_copy(step).wait_send()
        fresh_copy(step).wait_send()
        fresh_copy(step).wait_recv()

    each(ring, finish_far)
    each(SLOTS, finish_same)
    keep_fresh.wait()
    each(HALVES * SLOTS, lambda step: near_copy(step).wait_send())

    each(HALVES * SLOTS, lambda step: last_copy(step).wait_recv())
    total = last[:SLOTS] + last[SLOTS:]
    for pair in range(CLUSTERS // 2):
        rows = slice(pair * CHUNK, (pair + 1) * CHUNK)
        both = total[:, rows].reshape(nodes, 2 * PIECE).T
        shares[:, 2 * pair, :] = both[:PIECE]
        shares[:, 2 * pair + 1, :] = both[PIECE:]
    each(HALVES * SLOTS, lambda step: last_copy(step).wait_send())


def on_device(ring, turn_reach, regrets, pot, turn_cluster, bucket_map, codes, ranks):
    width = ranks.shape[1]
    depth = ring * LANES
    near = HALVES * SLOTS
    nodes = SLOTS * CHUNK
    chips = ring // CORES
    tile = (CLUSTERS // 2 * CHUNK, 2 * PIECE)
    vmem = pl.BlockSpec(memory_space=pltpu.VMEM)
    hbm = pl.BlockSpec(memory_space=pltpu.HBM)
    dma = pltpu.SemaphoreType.DMA
    fresh, shares = pl.pallas_call(
        kernel,
        out_shape=(
            jax.ShapeDtypeStruct((nodes, width), jnp.float32),
            jax.ShapeDtypeStruct((PIECE, CLUSTERS, nodes), jnp.float32),
        ),
        in_specs=[hbm, hbm, hbm, hbm, pl.BlockSpec(memory_space=pltpu.SMEM), hbm, hbm],
        out_specs=(hbm, vmem),
        scratch_shapes=[
            pltpu.VMEM((depth, width), jnp.bfloat16),
            pltpu.VMEM((width, depth), jnp.bfloat16),
            pltpu.VMEM((width, width), jnp.bfloat16),
            pltpu.VMEM((PIECE, CLUSTERS, nodes), jnp.bfloat16),
            pltpu.VMEM((PIECE, CLUSTERS, nodes), jnp.float32),
            pltpu.VMEM((SLOTS, *tile), jnp.bfloat16),
            pltpu.VMEM((1, nodes), jnp.float32),
            pltpu.VMEM((1, nodes), jnp.int32),
            pltpu.VMEM((1, width), jnp.int32),
            pltpu.VMEM((1, width), jnp.int32),
            pltpu.VMEM((SLOTS, CHUNK, 2 * LANES), jnp.float32),
            pltpu.VMEM((SLOTS, CHUNK, 2 * LANES), jnp.float32),
            pltpu.VMEM((SLOTS, CHUNK, width), jnp.float32),
            pltpu.VMEM((SLOTS, CHUNK, width), jnp.float32),
            pltpu.VMEM((near, *tile), jnp.bfloat16),
            pltpu.VMEM((1, LANES), jnp.int32),
            pltpu.VMEM((ring, 1, LANES), jnp.int32),
            pltpu.VMEM((ring, ROWS, LANES), jnp.bfloat16),
            pltpu.VMEM((chips, ROWS, CORES * LANES), jnp.bfloat16),
            pltpu.VMEM((ROWS, width), jnp.float32),
            pltpu.VMEM((ROWS, width), jnp.bfloat16),
            pltpu.VMEM((SLOTS, CHUNK, width), jnp.float32),
            pltpu.VMEM((ROWS, width), jnp.bfloat16),
            pltpu.VMEM((chips, ROWS, CORES * LANES), jnp.bfloat16),
            pltpu.VMEM((ring, ROWS, LANES), jnp.bfloat16),
            pltpu.VMEM((near, *tile), jnp.float32),
            pltpu.VMEM((near, *tile), jnp.float32),
            dma((6,)),
            dma((SLOTS,)),
            dma((SLOTS,)),
            dma((SLOTS,)),
            dma((SLOTS,)),
            dma((near,)),
            dma((near,)),
            dma((ring,)),
            dma((ring,)),
            dma((ring,)),
            dma((ring,)),
            dma((SLOTS,)),
            dma((SLOTS,)),
            dma((ring,)),
            dma((ring,)),
            dma((near,)),
            dma((near,)),
            dma,
        ],
        compiler_params=pltpu.CompilerParams(
            collective_id=0, has_side_effects=True, vmem_limit_bytes=48 * 2**20
        ),
    )(
        regrets[0, 0],
        turn_reach[0],
        pot[None],
        codes[None],
        turn_cluster,
        bucket_map,
        ranks,
    )
    return fresh[None, None], shares[None]


def solution(mesh):
    return jax.shard_map(
        functools.partial(on_device, mesh.shape["board"] // HALVES),
        mesh=mesh,
        in_specs=(
            P("pair", "board", None, "hist"),
            P("pair", "board", "hist", None),
            P("hist"),
            P("board"),
            P("board", None),
            P("hist"),
            P("board", None),
        ),
        out_specs=(P("pair", "board", "hist", None), P("pair", "board", None, "hist")),
        check_vma=False,
    )
```

time: 53.4 us -> 50.5 us (0.946)
  Pallas kernels: 47.4 us -> 44.2 us
    pallas_call x1, Pallas kernels: 47.4 us -> 44.2 us  [on_device(): pl.pallas_call(kernel, out_shape=(jax.ShapeDtypeStruct((nodes, width), jn...]
    unnamed x13 -> x14, local copies, waits for them, and re-layouts: 4.12 us -> 4.68 us
where the time goes in v2:
time: 50.5 us; the launch traced here: 50.2 us
  Pallas kernels  44.2 us (88%)
  local copies, waits for them, and re-layouts  4.68 us (9%)
  between operations  1.33 us (3%)
    pallas_call x1, Pallas kernels, on_device(): pl.pallas_call(kernel, out_shape=(jax.ShapeDtypeStruct((nodes, width), jn...  44.2 us
    unnamed x14, local copies, waits for them, and re-layouts  4.68 us

profile of v2, /device:TPU:1, one launch (start us, length us, event | category | flops | bytes accessed | tf_op | source)
XLA Modules:
  0.0 50.2 jit_solution(8424172960518150007)
XLA Ops:
  0.6 0.0 copy-start.2
  1.3 0.0 copy-start.4
  1.3 0.0 copy-start.5
  1.3 0.0 copy-done.2
  1.3 0.6 %copy-done.4 = f32[64]{0:T(128)S(1)} copy-done((f32[64]{0:T(128)S(1)}, f32[64]{0:T(128)}, u32[]{:S(2)}) %copy-start.4) | copy-done | bytes 280
  2.0 0.0 copy-done.5
  2.0 0.0 copy-start
  2.0 1.0 %copy-done = f32[1,1,64,2048]{3,2,1,0:T(8,128)S(1)} copy-done((f32[1,1,64,2048]{3,2,1,0:T(8,128)S(1)}, f32[1,1,64,2048]{3,2,1,0:T(8,128)}, u32[]{:S(2)}) %copy-start) | copy-done | bytes 524312
  3.0 0.0 copy-start.1
  3.0 0.8 %copy-done.1 = bf16[1,64,4,64]{3,2,1,0:T(4,128)(2,1)S(1)} copy-done((bf16[1,64,4,64]{3,2,1,0:T(4,128)(2,1)S(1)}, bf16[1,64,4,64]{3,2,1,0:T(4,128)(2,1)}, u32[]{:S(2)}) %copy-start.1) | copy-done | bytes 32792
  3.9 0.0 copy-start.3
  3.9 0.7 %copy-done.3 = s32[1,2048]{1,0:T(1,128)S(1)} copy-done((s32[1,2048]{1,0:T(1,128)S(1)}, s32[1,2048]{1,0:T(1,128)}, u32[]{:S(2)}) %copy-start.3) | copy-done | bytes 8216
  4.6 44.2 %shard_map.86 = (f32[64,2048]{1,0:T(8,128)S(1)}, f32[64,4,64]{2,1,0:T(4,128)S(1)}) custom-call(f32[64,2048]{1,0:T(8,128)S(1)} %bitcast.6, bf16[64,4,64]{2,1,0:T(4,128)(2,1)S(1)} %bitcast.9, f32[1,64]{1,0:T(1,128)S(1)} %bitcast.10, s32[1,64]{1,0:T(1,128)S(1)} %bitcast.11, s32[1]{0:T(128)S(6)} %copy.11.cluster, s32[1,2048]{1,0:T(1,128)S(1)} %copy-done.2, ...), custom_call_target="tpu_custom_call" | custom-call | tf_op jit(solution)/shard_map/pallas_call | solution.py:485
  48.8 0.8 %copy.12 = f32[1,1,64,2048]{3,2,1,0:T(8,128)} copy(f32[1,1,64,2048]{3,2,1,0:T(8,128)S(1)} %bitcast.7) | data formatting | bytes 1048576
  49.6 0.7 %copy.13 = f32[1,64,4,64]{3,2,1,0:T(4,128)} copy(f32[1,64,4,64]{3,2,1,0:T(4,128)S(1)} %bitcast.8) | data formatting | bytes 131072
Async XLA Ops:
  0.6 0.7 %copy-start.2 = (s32[1,2048]{1,0:T(1,128)S(1)}, s32[1,2048]{1,0:T(1,128)}, u32[]{:S(2)}) copy-start(s32[1,2048]{1,0:T(1,128)} %mapping.1) | copy-start | bytes 24580
  1.3 0.7 %copy-start.4 = (f32[64]{0:T(128)S(1)}, f32[64]{0:T(128)}, u32[]{:S(2)}) copy-start(f32[64]{0:T(128)} %param.9) | copy-start | bytes 772
  1.3 0.7 %copy-start.5 = (s32[64]{0:T(128)S(1)}, s32[64]{0:T(128)}, u32[]{:S(2)}) copy-start(s32[64]{0:T(128)} %param.12) | copy-start | bytes 772
  2.0 1.0 %copy-start = (f32[1,1,64,2048]{3,2,1,0:T(8,128)S(1)}, f32[1,1,64,2048]{3,2,1,0:T(8,128)}, u32[]{:S(2)}) copy-start(f32[1,1,64,2048]{3,2,1,0:T(8,128)} %param.8) | copy-start | bytes 1572868
  3.0 0.8 %copy-start.1 = (bf16[1,64,4,64]{3,2,1,0:T(4,128)(2,1)S(1)}, bf16[1,64,4,64]{3,2,1,0:T(4,128)(2,1)}, u32[]{:S(2)}) copy-start(bf16[1,64,4,64]{3,2,1,0:T(4,128)(2,1)} %param.7) | copy-start | bytes 98308
  3.9 0.7 %copy-start.3 = (s32[1,2048]{1,0:T(1,128)S(1)}, s32[1,2048]{1,0:T(1,128)}, u32[]{:S(2)}) copy-start(s32[1,2048]{1,0:T(1,128)} %ranks.1) | copy-start | bytes 24580

commit v3 on v2

--- a/solution.py
+++ b/solution.py
@@ -19,6 +19,13 @@
 CORES = 2
 LANES = 128
 MESH = pl.DeviceIdType.MESH
+SMALL = jnp.float8_e4m3fn
+
+
+def times(rows, matrix):
+    return lax.dot_general(
+        rows, matrix, (((1,), (0,)), ((), ())), preferred_element_type=jnp.float32
+    )
 
 
 def kernel(
@@ -266,7 +273,6 @@
     each(HALVES * SLOTS, lambda step: near_copy(step).start())
     each(ring, lambda step: cluster_copy(step).start())
     each(SLOTS, lambda step: meta_copy(step).start())
-    each(SLOTS, lambda step: regret_copy(step).start())
 
     for fetch in fetches[3:5]:
         fetch.wait()
@@ -278,10 +284,12 @@
         for tile in range(width // LANES):
             span = slice(tile * LANES, (tile + 1) * LANES)
             sign = jnp.minimum(jnp.maximum(rank_wide[:, span] - rank_column, -1.0), 1.0)
-            strength[lanes_of(block), span] = sign.astype(jnp.bfloat16)
+            strength[lanes_of(block), span] = sign.astype(SMALL)
         return carry
 
     lax.fori_loop(0, width // LANES, build_strength, 0)
+
+    each(SLOTS, lambda step: regret_copy(step).start())
 
     each(HALVES * SLOTS, lambda step: near_copy(step).wait_recv())
     each(ring, lambda step: cluster_copy(step).wait_recv())
@@ -322,7 +330,7 @@
         for tile in range(width // LANES):
             span = slice(tile * LANES, (tile + 1) * LANES)
             hit = jnp.where(map_wide[:, span] == index, 1.0, 0.0)
-            onehot[lanes_of(block), span] = hit.astype(jnp.bfloat16)
+            onehot[lanes_of(block), span] = hit.astype(SMALL)
         return carry
 
     lax.fori_loop(0, tiles, build_onehot, 0)
@@ -334,7 +342,7 @@
         for tile in range(tiles):
             span = slice(tile * LANES, (tile + 1) * LANES)
             hit = jnp.where(map_column == index + tile * LANES, 1.0, 0.0)
-            spread[lanes_of(block), span] = hit.astype(jnp.bfloat16)
+            spread[lanes_of(block), span] = hit.astype(SMALL)
         return carry
 
     lax.fori_loop(0, width // LANES, build_spread, 0)
@@ -353,7 +361,7 @@
                 sigma[who * ACTIONS + act, :, span] = (positive[act] + SMOOTH) * inverse
 
     totals = jnp.zeros((ROWS, 1), jnp.float32)
-    for turn_of, distance in enumerate(inward):
+    for turn_of, distance in enumerate([0] + outward[:-1]):
         if turn_of == chips // 2:
             each(SLOTS, lambda step: regret_copy(step).wait_recv())
             fetches[5].wait()
@@ -366,7 +374,7 @@
         rows = pl.ds(pl.multiple_of(source * CORES * LANES, CORES * LANES), CORES * LANES)
         panel = far[source]
         for span in spans:
-            now = jnp.dot(panel, onehot[rows, span], preferred_element_type=jnp.float32)
+            now = times(panel, onehot[rows, span])
             if turn_of > 0:
                 now = now + lifted[:, span]
             if turn_of < chips - 1:
@@ -392,23 +400,11 @@
     show_wide = jnp.concatenate([code_here] * repeats, axis=1) == 2.0
 
     for span in spans:
-        equity = jnp.dot(reach[...], strength[:, span], preferred_element_type=jnp.float32)
+        equity = times(reach[...], strength[:, span])
         value = jnp.where(show_wide, pot_wide * opponent(equity), fold_wide)
         updated[:, :, span] = value.reshape(SLOTS, CHUNK, step_width)
         share = sigma[:, :, span].reshape(ROWS, step_width) * value
         weighted[:, span] = share.astype(jnp.bfloat16)
-
-    for distance in outward:
-        there = (chip + distance) % chips
-        columns_there = pl.ds(pl.multiple_of(there * CORES * LANES, CORES * LANES), CORES * LANES)
-        block = jnp.dot(
-            weighted[...], spread[:, columns_there], preferred_element_type=jnp.float32
-        )
-        back_out[there] = block.astype(jnp.bfloat16)
-        for step in range(distance * CORES, (distance + 1) * CORES):
-            if step > 0:
-                back_copy(step).start()
-    back[place] = back_out[chip, :, lanes_of(core)]
 
     def renew(tile, carry):
         span = lanes_of(tile)
@@ -421,10 +417,21 @@
                 updated[index, :, span] = (regret[index, :, span] + now) - node
         return carry
 
-    lax.fori_loop(0, width // LANES, renew, 0)
-    each(SLOTS, lambda step: fresh_copy(step).start())
     keep_fresh = pltpu.make_async_copy(updated.at[slot], fresh.at[chunk_of(chunk)], local_sem)
-    keep_fresh.start()
+
+    for turn_of, distance in enumerate(outward):
+        if turn_of == chips // 2:
+            lax.fori_loop(0, width // LANES, renew, 0)
+            each(SLOTS, lambda step: fresh_copy(step).start())
+            keep_fresh.start()
+        there = (chip + distance) % chips
+        columns_there = pl.ds(pl.multiple_of(there * CORES * LANES, CORES * LANES), CORES * LANES)
+        block = times(weighted[...], spread[:, columns_there])
+        back_out[there] = block.astype(jnp.bfloat16)
+        for step in range(distance * CORES, (distance + 1) * CORES):
+            if step > 0:
+                back_copy(step).start()
+    back[place] = back_out[chip, :, lanes_of(core)]
 
     held = [jnp.zeros((ROWS, LANES), jnp.float32) for unused in range(CLUSTERS)]
     for distance in inward:
@@ -491,9 +498,9 @@
         in_specs=[hbm, hbm, hbm, hbm, pl.BlockSpec(memory_space=pltpu.SMEM), hbm, hbm],
         out_specs=(hbm, vmem),
         scratch_shapes=[
-            pltpu.VMEM((depth, width), jnp.bfloat16),
-            pltpu.VMEM((width, depth), jnp.bfloat16),
-            pltpu.VMEM((width, width), jnp.bfloat16),
+            pltpu.VMEM((depth, width), SMALL),
+            pltpu.VMEM((width, depth), SMALL),
+            pltpu.VMEM((width, width), SMALL),
             pltpu.VMEM((PIECE, CLUSTERS, nodes), jnp.bfloat16),
             pltpu.VMEM((PIECE, CLUSTERS, nodes), jnp.float32),
             pltpu.VMEM((SLOTS, *tile), jnp.bfloat16),
@@ -538,16 +545,15 @@
             dma,
         ],
         compiler_params=pltpu.CompilerParams(
-            collective_id=0, has_side_effects=True, vmem_limit_bytes=48 * 2**20
+            collective_id=0, has_side_effects=True, vmem_limit_bytes=32 * 2**20
         ),
     )(
-        regrets[0, 0],
-        turn_reach[0],
-        pot[None],
-        codes[None],
+        *(
+            pltpu.with_memory_space_constraint(x, pltpu.HBM)
+            for x in (regrets[0, 0], turn_reach[0], pot[None], codes[None])
+        ),
         turn_cluster,
-        bucket_map,
-        ranks,
+        *(pltpu.with_memory_space_constraint(x, pltpu.HBM) for x in (bucket_map, ranks)),
     )
     return fresh[None, None], shares[None]
 

time: 50.5 us -> 42.9 us (0.85)
  Pallas kernels: 44.2 us -> 40 us
  local copies, waits for them, and re-layouts: 4.68 us -> 1.45 us
    pallas_call x1, Pallas kernels: 44.2 us -> 40 us  [on_device(): pl.pallas_call(kernel, out_shape=(jax.ShapeDtypeStruct((nodes, width), jn...]
    unnamed x14 -> x2, local copies, waits for them, and re-layouts: 4.68 us -> 1.45 us
where the time goes in v3:
time: 42.9 us; the launch traced here: 42.8 us
  Pallas kernels  40 us (93%)
  local copies, waits for them, and re-layouts  1.45 us (3%)
  between operations  1.29 us (3%)
    pallas_call x1, Pallas kernels, on_device(): pl.pallas_call(kernel, out_shape=(jax.ShapeDtypeStruct((nodes, width), jn...  40 us
    unnamed x2, local copies, waits for them, and re-layouts  1.45 us

profile of v3, /device:TPU:1, one launch (start us, length us, event | category | flops | bytes accessed | tf_op | source)
XLA Modules:
  0.0 42.8 jit_solution(18061497978705669704)
XLA Ops:
  1.3 40.0 %shard_map.86 = (f32[64,2048]{1,0:T(8,128)S(1)}, f32[64,4,64]{2,1,0:T(4,128)S(1)}) custom-call(f32[64,2048]{1,0:T(8,128)} %bitcast.8, bf16[64,4,64]{2,1,0:T(4,128)(2,1)} %bitcast.9, f32[1,64]{1,0:T(1,128)} %bitcast.10, s32[1,64]{1,0:T(1,128)} %bitcast.11, s32[1]{0:T(128)S(6)} %copy.11.cluster, s32[1,2048]{1,0:T(1,128)} %mapping.1, s32[1,2048]{1,0:T(1,128)} %ranks.1), custom_call_target="tpu_custom_call" | custom-call | tf_op jit(solution)/shard_map/pallas_call | solution.py:492
  41.3 0.8 %copy.12 = f32[1,1,64,2048]{3,2,1,0:T(8,128)} copy(f32[1,1,64,2048]{3,2,1,0:T(8,128)S(1)} %bitcast.6) | data formatting | bytes 1048576
  42.1 0.7 %copy.13 = f32[1,64,4,64]{3,2,1,0:T(4,128)} copy(f32[1,64,4,64]{3,2,1,0:T(4,128)S(1)} %bitcast.7) | data formatting | bytes 131072

commit v4 on v3

--- a/solution.py
+++ b/solution.py
@@ -82,10 +82,9 @@
     back_recv,
     last_send,
     last_recv,
-    local_sem,
 ):
     width = ranks.shape[1]
-    ring = far_send.shape[0]
+    ring = back.shape[0]
     chips = ring // CORES
     board = lax.axis_index("board")
     action = lax.axis_index("hist")
@@ -96,7 +95,6 @@
     core = place % CORES
     chunk = action * PLAYERS + player
     slot = player * ACTIONS + action
-    group = half * SLOTS + chunk
     scale = width ** (-0.5)
     inward = [(i + 1) // 2 if i % 2 else (chips - i // 2) % chips for i in range(chips)]
     outward = inward[::-1]
@@ -106,14 +104,30 @@
         return other, {"board": board, "hist": other // PLAYERS, "pair": other % PLAYERS}
 
     def near_peer(step):
-        other = (group + step) % (HALVES * SLOTS)
-        their_chunk = other % SLOTS
+        their_half = (half + step // SLOTS) % HALVES
+        their_action = (action + step % SLOTS // PLAYERS) % ACTIONS
+        their_player = (player + step) % PLAYERS
+        their_chunk = their_action * PLAYERS + their_player
+        their_slot = their_player * ACTIONS + their_action
         target = {
-            "board": (other // SLOTS) * ring + place,
-            "hist": their_chunk // PLAYERS,
-            "pair": their_chunk % PLAYERS,
+            "board": their_half * ring + place,
+            "hist": their_action,
+            "pair": their_player,
         }
-        return other, target
+        return their_half, their_chunk, their_slot, target
+
+    def hops(step):
+        along = step % SLOTS // PLAYERS
+        across = 1 if step % PLAYERS else 2 * (step // SLOTS)
+        return min(along, ACTIONS - along) + across
+
+    near_steps = sorted(range(1, HALVES * SLOTS), key=hops, reverse=True)
+    far_steps = [
+        step
+        for distance in outward
+        for step in range(distance * CORES, (distance + 1) * CORES)
+        if step > 0
+    ]
 
     def far_peer(step):
         there = (chip + step // CORES) % chips
@@ -128,45 +142,51 @@
     def chunk_of(index):
         return pl.ds(pl.multiple_of(index * CHUNK, CHUNK), CHUNK)
 
-    def remote(src, dst, send, recv, step, target):
+    def remote(src, dst, send, recv, target):
         return pltpu.make_async_remote_copy(
             src_ref=src,
             dst_ref=dst,
-            send_sem=send.at[step],
-            recv_sem=recv.at[step],
+            send_sem=send,
+            recv_sem=recv,
             device_id=target,
             device_id_type=MESH,
         )
+
+    def await_bytes(buffer, semaphore):
+        pltpu.make_async_copy(buffer, buffer, semaphore).wait()
 
     def regret_copy(step):
         other, target = same_board(step)
         return remote(
-            regrets.at[chunk_of(other)], regret.at[slot], regret_send, regret_recv, step, target
+            regrets.at[chunk_of(other)], regret.at[slot], regret_send, regret_recv, target
         )
 
     def meta_copy(step):
         other, target = same_board(step)
-        return remote(meta_out.at[other], meta.at[slot], meta_send, meta_recv, step, target)
+        return remote(meta_out.at[other], meta.at[slot], meta_send, meta_recv, target)
 
     def near_copy(step):
-        other, target = near_peer(step)
+        their_half, their_chunk, their_slot, target = near_peer(step)
         return remote(
-            turn.at[other % SLOTS],
+            turn.at[their_chunk],
             near.at[half * SLOTS + slot],
             near_send,
             near_recv,
-            step,
             target,
         )
 
     def cluster_copy(step):
         there, mate, other, target = far_peer(step)
-        return remote(cluster_out, clusters.at[place], cluster_send, cluster_recv, step, target)
+        return remote(cluster_out, clusters.at[place], cluster_send, cluster_recv, target)
 
     def far_copy(step):
         there, mate, other, target = far_peer(step)
         return remote(
-            far_out.at[other], far.at[chip, :, lanes_of(core)], far_send, far_recv, step, target
+            far_out.at[other],
+            far.at[chip, :, lanes_of(core)],
+            far_send,
+            far_recv.at[step // CORES],
+            target,
         )
 
     def fresh_copy(step):
@@ -177,7 +197,6 @@
             fresh.at[chunk_of(chunk)],
             fresh_send,
             fresh_recv,
-            step,
             target,
         )
 
@@ -188,20 +207,16 @@
             back.at[place],
             back_send,
             back_recv,
-            step,
             target,
         )
 
     def last_copy(step):
-        other, target = near_peer(step)
-        their_chunk = other % SLOTS
-        their_slot = (their_chunk % PLAYERS) * ACTIONS + their_chunk // PLAYERS
+        their_half, their_chunk, their_slot, target = near_peer(step)
         return remote(
-            last_out.at[(other // SLOTS) * SLOTS + their_slot],
+            last_out.at[their_half * SLOTS + their_slot],
             last.at[half * SLOTS + chunk],
             last_send,
             last_recv,
-            step,
             target,
         )
 
@@ -212,34 +227,33 @@
 
         lax.fori_loop(1, count, body, 0)
 
-    fetches = [
-        pltpu.make_async_copy(src, dst, fetch_sem.at[index])
-        for index, (src, dst) in enumerate(
-            [
-                (turn_reach, turn_raw),
-                (pot, pot_row),
-                (codes, code_row),
-                (ranks, rank_row),
-                (mapping, map_row),
-                (regrets.at[chunk_of(chunk)], regret.at[slot]),
-            ]
-        )
+    sources = [
+        (turn_reach, turn_raw, fetch_sem.at[0]),
+        (pot, pot_row, fetch_sem.at[1]),
+        (codes, code_row, fetch_sem.at[2]),
+        (ranks, rank_row, fetch_sem.at[3]),
+        (mapping, map_row, fetch_sem.at[4]),
+        (regrets.at[chunk_of(chunk)], regret.at[slot], regret_recv),
     ]
-    for fetch in fetches:
+    fetches = [pltpu.make_async_copy(*source) for source in sources]
+    fetches[0].start()
+
+    barrier = pltpu.get_barrier_semaphore()
+
+    def greet_near(step):
+        target = near_peer(step)[-1]
+        pl.semaphore_signal(barrier, inc=1, device_id=target, device_id_type=MESH)
+
+    def greet_far(step):
+        target = far_peer(step)[-1]
+        pl.semaphore_signal(barrier, inc=1, device_id=target, device_id_type=MESH)
+
+    for step in near_steps:
+        greet_near(step)
+    for step in far_steps:
+        greet_far(step)
+    for fetch in fetches[1:]:
         fetch.start()
-
-    barrier = pltpu.get_barrier_semaphore()
-
-    def greet_near(step):
-        other, target = near_peer(step)
-        pl.semaphore_signal(barrier, inc=1, device_id=target, device_id_type=MESH)
-
-    def greet_far(step):
-        there, mate, other, target = far_peer(step)
-        pl.semaphore_signal(barrier, inc=1, device_id=target, device_id_type=MESH)
-
-    each(ring, greet_far)
-    each(HALVES * SLOTS, greet_near)
 
     own_cluster = jnp.full((1, LANES), cluster[0], jnp.int32)
     cluster_out[...] = own_cluster
@@ -270,8 +284,10 @@
     meta[slot] = meta_out[chunk]
     pl.semaphore_wait(barrier, HALVES * SLOTS - 1 + ring - 1)
 
-    each(HALVES * SLOTS, lambda step: near_copy(step).start())
-    each(ring, lambda step: cluster_copy(step).start())
+    for step in near_steps:
+        near_copy(step).start()
+    for step in far_steps:
+        cluster_copy(step).start()
     each(SLOTS, lambda step: meta_copy(step).start())
 
     for fetch in fetches[3:5]:
@@ -291,8 +307,8 @@
 
     each(SLOTS, lambda step: regret_copy(step).start())
 
-    each(HALVES * SLOTS, lambda step: near_copy(step).wait_recv())
-    each(ring, lambda step: cluster_copy(step).wait_recv())
+    await_bytes(near.at[pl.ds(1, HALVES * SLOTS - 1)], near_recv)
+    await_bytes(clusters.at[pl.ds(1, ring - 1)], cluster_recv)
     low = lax.broadcasted_iota(jnp.int32, (SLOTS, CHUNK, LANES), 2) < PIECE
     parts = []
     lower = near[:SLOTS].astype(jnp.float32)
@@ -311,12 +327,10 @@
             result = jnp.where(wanted == index, panels[index], result)
         return result.astype(jnp.bfloat16)
 
-    for distance in outward:
-        for step in range(distance * CORES, (distance + 1) * CORES):
-            if step > 0:
-                there, mate, other, target = far_peer(step)
-                far_out[other] = choose(other)
-                far_copy(step).start()
+    for step in far_steps:
+        other = far_peer(step)[2]
+        far_out[other] = choose(other)
+        far_copy(step).start()
     far[chip, :, lanes_of(core)] = choose(place)
 
     bucket = map_row[...]
@@ -363,13 +377,11 @@
     totals = jnp.zeros((ROWS, 1), jnp.float32)
     for turn_of, distance in enumerate([0] + outward[:-1]):
         if turn_of == chips // 2:
-            each(SLOTS, lambda step: regret_copy(step).wait_recv())
-            fetches[5].wait()
+            await_bytes(regret, regret_recv)
             for span in spans:
                 match(span)
-        for step in range(distance * CORES, (distance + 1) * CORES):
-            if step > 0:
-                far_copy(step).wait_recv()
+        arrived = far.at[0, :, pl.ds(0, LANES)] if distance == 0 else far.at[0]
+        await_bytes(arrived, far_recv.at[distance])
         source = (chip + chips - distance) % chips
         rows = pl.ds(pl.multiple_of(source * CORES * LANES, CORES * LANES), CORES * LANES)
         panel = far[source]
@@ -387,7 +399,7 @@
     def opponent(rows):
         return jnp.concatenate([rows[ROWS // 2 :], rows[: ROWS // 2]], axis=0)
 
-    each(SLOTS, lambda step: meta_copy(step).wait_recv())
+    await_bytes(meta.at[pl.ds(1, SLOTS - 1)], meta_recv)
     pot_here = meta[:, :, :LANES].reshape(ROWS, LANES) * scale
     code_here = meta[:, :, LANES:].reshape(ROWS, LANES)
     row = lax.broadcasted_iota(jnp.int32, (ROWS, LANES), 0)
@@ -417,7 +429,7 @@
                 updated[index, :, span] = (regret[index, :, span] + now) - node
         return carry
 
-    keep_fresh = pltpu.make_async_copy(updated.at[slot], fresh.at[chunk_of(chunk)], local_sem)
+    keep_fresh = pltpu.make_async_copy(updated.at[slot], fresh.at[chunk_of(chunk)], fresh_recv)
 
     for turn_of, distance in enumerate(outward):
         if turn_of == chips // 2:
@@ -434,15 +446,12 @@
     back[place] = back_out[chip, :, lanes_of(core)]
 
     held = [jnp.zeros((ROWS, LANES), jnp.float32) for unused in range(CLUSTERS)]
-    for distance in inward:
-        for step in range(distance * CORES, (distance + 1) * CORES):
-            if step > 0:
-                back_copy(step).wait_recv()
-            source = ((chip + chips - distance) % chips) * CORES + (core + step) % CORES
-            block = back[source].astype(jnp.float32)
-            theirs = clusters[source]
-            for index in range(CLUSTERS):
-                held[index] = held[index] + jnp.where(theirs == index, block, 0.0)
+    await_bytes(back.at[pl.ds(1, ring - 1)], back_recv)
+    for source in range(ring):
+        block = back[source].astype(jnp.float32)
+        theirs = clusters[source]
+        for index in range(CLUSTERS):
+            held[index] = held[index] + jnp.where(theirs == index, block, 0.0)
     held = [part.reshape(SLOTS, CHUNK, LANES) for part in held]
     for pair in range(CLUSTERS // 2):
         rows = slice(pair * CHUNK, (pair + 1) * CHUNK)
@@ -450,33 +459,27 @@
         last_out[:SLOTS, rows] = jnp.where(low, first, pltpu.roll(second, PIECE, 2))
         last_out[SLOTS:, rows] = jnp.where(low, pltpu.roll(first, PIECE, 2), second)
 
-    each(HALVES * SLOTS, lambda step: last_copy(step).start())
+    for step in near_steps:
+        last_copy(step).start()
     last[half * SLOTS + chunk] = last_out[half * SLOTS + slot]
 
-    def finish_far(step):
-        cluster_copy(step).wait_send()
-        far_copy(step).wait_send()
-        back_copy(step).wait_send()
-
-    def finish_same(step):
-        regret_copy(step).wait_send()
-        meta_copy(step).wait_send()
-        fresh_copy(step).wait_send()
-        fresh_copy(step).wait_recv()
-
-    each(ring, finish_far)
-    each(SLOTS, finish_same)
-    keep_fresh.wait()
-    each(HALVES * SLOTS, lambda step: near_copy(step).wait_send())
-
-    each(HALVES * SLOTS, lambda step: last_copy(step).wait_recv())
+    await_bytes(clusters.at[pl.ds(1, ring - 1)], cluster_send)
+    await_bytes(far_out.at[pl.ds(1, ring - 1)], far_send)
+    await_bytes(back.at[pl.ds(1, ring - 1)], back_send)
+    await_bytes(regret.at[pl.ds(1, SLOTS - 1)], regret_send)
+    await_bytes(meta.at[pl.ds(1, SLOTS - 1)], meta_send)
+    await_bytes(near.at[pl.ds(1, HALVES * SLOTS - 1)], near_send)
+    await_bytes(updated.at[pl.ds(1, SLOTS - 1)], fresh_send)
+    await_bytes(updated, fresh_recv)
+
+    await_bytes(last.at[pl.ds(1, HALVES * SLOTS - 1)], last_recv)
     total = last[:SLOTS] + last[SLOTS:]
     for pair in range(CLUSTERS // 2):
         rows = slice(pair * CHUNK, (pair + 1) * CHUNK)
         both = total[:, rows].reshape(nodes, 2 * PIECE).T
         shares[:, 2 * pair, :] = both[:PIECE]
         shares[:, 2 * pair + 1, :] = both[PIECE:]
-    each(HALVES * SLOTS, lambda step: last_copy(step).wait_send())
+    await_bytes(last.at[pl.ds(1, HALVES * SLOTS - 1)], last_send)
 
 
 def on_device(ring, turn_reach, regrets, pot, turn_cluster, bucket_map, codes, ranks):
@@ -525,23 +528,22 @@
             pltpu.VMEM((ring, ROWS, LANES), jnp.bfloat16),
             pltpu.VMEM((near, *tile), jnp.float32),
             pltpu.VMEM((near, *tile), jnp.float32),
-            dma((6,)),
-            dma((SLOTS,)),
-            dma((SLOTS,)),
-            dma((SLOTS,)),
-            dma((SLOTS,)),
-            dma((near,)),
-            dma((near,)),
-            dma((ring,)),
-            dma((ring,)),
-            dma((ring,)),
-            dma((ring,)),
-            dma((SLOTS,)),
-            dma((SLOTS,)),
-            dma((ring,)),
-            dma((ring,)),
-            dma((near,)),
-            dma((near,)),
+            dma((5,)),
+            dma,
+            dma,
+            dma,
+            dma,
+            dma,
+            dma,
+            dma,
+            dma,
+            dma,
+            dma((chips,)),
+            dma,
+            dma,
+            dma,
+            dma,
+            dma,
             dma,
         ],
         compiler_params=pltpu.CompilerParams(

time: 42.9 us -> 40.8 us (0.951)
  Pallas kernels: 40 us -> 38 us
    pallas_call x1, Pallas kernels: 40 us -> 38 us  [on_device(): pl.pallas_call(kernel, out_shape=(jax.ShapeDtypeStruct((nodes, width), jn...]
where the time goes in v4:
time: 40.8 us; the launch traced here: 40.7 us
  Pallas kernels  38 us (93%)
  local copies, waits for them, and re-layouts  1.45 us (4%)
  between operations  1.29 us (3%)
    pallas_call x1, Pallas kernels, on_device(): pl.pallas_call(kernel, out_shape=(jax.ShapeDtypeStruct((nodes, width), jn...  38 us
    unnamed x2, local copies, waits for them, and re-layouts  1.45 us

profile of v4, /device:TPU:1, one launch (start us, length us, event | category | flops | bytes accessed | tf_op | source)
XLA Modules:
  0.0 40.7 jit_solution(4168401287683651957)
XLA Ops:
  1.3 38.0 %shard_map.86 = (f32[64,2048]{1,0:T(8,128)S(1)}, f32[64,4,64]{2,1,0:T(4,128)S(1)}) custom-call(f32[64,2048]{1,0:T(8,128)} %bitcast.8, bf16[64,4,64]{2,1,0:T(4,128)(2,1)} %bitcast.9, f32[1,64]{1,0:T(1,128)} %bitcast.10, s32[1,64]{1,0:T(1,128)} %bitcast.11, s32[1]{0:T(128)S(6)} %copy.11.cluster, s32[1,2048]{1,0:T(1,128)} %mapping.1, s32[1,2048]{1,0:T(1,128)} %ranks.1), custom_call_target="tpu_custom_call" | custom-call | tf_op jit(solution)/shard_map/pallas_call | solution.py:495
  39.2 0.8 %copy.12 = f32[1,1,64,2048]{3,2,1,0:T(8,128)} copy(f32[1,1,64,2048]{3,2,1,0:T(8,128)S(1)} %bitcast.6) | data formatting | bytes 1048576
  40.0 0.7 %copy.13 = f32[1,64,4,64]{3,2,1,0:T(4,128)} copy(f32[1,64,4,64]{3,2,1,0:T(4,128)S(1)} %bitcast.7) | data formatting | bytes 131072

commit v5 on v4

--- a/solution.py
+++ b/solution.py
@@ -200,8 +200,8 @@
             target,
         )
 
-    def back_copy(step):
-        there, mate, other, target = far_peer(step)
+    def back_copy(there, mate):
+        target = {"board": half * ring + there * CORES + mate, "hist": action, "pair": player}
         return remote(
             back_out.at[there, :, lanes_of(mate)],
             back.at[place],
@@ -210,8 +210,15 @@
             target,
         )
 
-    def last_copy(step):
-        their_half, their_chunk, their_slot, target = near_peer(step)
+    def last_copy(there):
+        their_half, rest = there // SLOTS, there % SLOTS
+        their_action, their_player = rest // PLAYERS, rest % PLAYERS
+        their_slot = their_player * ACTIONS + their_action
+        target = {
+            "board": their_half * ring + place,
+            "hist": their_action,
+            "pair": their_player,
+        }
         return remote(
             last_out.at[their_half * SLOTS + their_slot],
             last.at[half * SLOTS + chunk],
@@ -431,18 +438,20 @@
 
     keep_fresh = pltpu.make_async_copy(updated.at[slot], fresh.at[chunk_of(chunk)], fresh_recv)
 
-    for turn_of, distance in enumerate(outward):
+    for turn_of, there in enumerate([0, 1, 2, 3, 4, 5, 6, 7]):
         if turn_of == chips // 2:
             lax.fori_loop(0, width // LANES, renew, 0)
             each(SLOTS, lambda step: fresh_copy(step).start())
             keep_fresh.start()
-        there = (chip + distance) % chips
-        columns_there = pl.ds(pl.multiple_of(there * CORES * LANES, CORES * LANES), CORES * LANES)
+        columns_there = slice(there * CORES * LANES, (there + 1) * CORES * LANES)
         block = times(weighted[...], spread[:, columns_there])
         back_out[there] = block.astype(jnp.bfloat16)
-        for step in range(distance * CORES, (distance + 1) * CORES):
-            if step > 0:
-                back_copy(step).start()
+        for mate in reversed(range(CORES)):
+
+            @pl.when(place != there * CORES + mate)
+            def send_back(there=there, mate=mate):
+                back_copy(there, mate).start()
+
     back[place] = back_out[chip, :, lanes_of(core)]
 
     held = [jnp.zeros((ROWS, LANES), jnp.float32) for unused in range(CLUSTERS)]
@@ -459,8 +468,15 @@
         last_out[:SLOTS, rows] = jnp.where(low, first, pltpu.roll(second, PIECE, 2))
         last_out[SLOTS:, rows] = jnp.where(low, pltpu.roll(first, PIECE, 2), second)
 
-    for step in near_steps:
-        last_copy(step).start()
+    def lateness(there):
+        return there // SLOTS * PLAYERS + there % PLAYERS + there % SLOTS // PLAYERS
+
+    for there in sorted(range(HALVES * SLOTS), key=lateness):
+
+        @pl.when(there != half * SLOTS + chunk)
+        def send_last(there=there):
+            last_copy(there).start()
+
     last[half * SLOTS + chunk] = last_out[half * SLOTS + slot]
 
     await_bytes(clusters.at[pl.ds(1, ring - 1)], cluster_send)

time: 40.8 us -> 39 us (0.956)
  Pallas kernels: 38 us -> 36.2 us
    pallas_call x1, Pallas kernels: 38 us -> 36.2 us  [on_device(): pl.pallas_call(kernel, out_shape=(jax.ShapeDtypeStruct((nodes, width), jn...]
where the time goes in v5:
time: 39 us; the launch traced here: 38.9 us
  Pallas kernels  36.2 us (93%)
  local copies, waits for them, and re-layouts  1.45 us (4%)
  between operations  1.29 us (3%)
    pallas_call x1, Pallas kernels, on_device(): pl.pallas_call(kernel, out_shape=(jax.ShapeDtypeStruct((nodes, width), jn...  36.2 us
    unnamed x2, local copies, waits for them, and re-layouts  1.45 us

profile of v5, /device:TPU:1, one launch (start us, length us, event | category | flops | bytes accessed | tf_op | source)
XLA Modules:
  0.0 38.9 jit_solution(10484498032862521088)
XLA Ops:
  1.3 36.2 %shard_map.86 = (f32[64,2048]{1,0:T(8,128)S(1)}, f32[64,4,64]{2,1,0:T(4,128)S(1)}) custom-call(f32[64,2048]{1,0:T(8,128)} %bitcast.8, bf16[64,4,64]{2,1,0:T(4,128)(2,1)} %bitcast.9, f32[1,64]{1,0:T(1,128)} %bitcast.10, s32[1,64]{1,0:T(1,128)} %bitcast.11, s32[1]{0:T(128)S(6)} %copy.11.cluster, s32[1,2048]{1,0:T(1,128)} %mapping.1, s32[1,2048]{1,0:T(1,128)} %ranks.1), custom_call_target="tpu_custom_call" | custom-call | tf_op jit(solution)/shard_map/pallas_call | solution.py:511
  37.4 0.8 %copy.12 = f32[1,1,64,2048]{3,2,1,0:T(8,128)} copy(f32[1,1,64,2048]{3,2,1,0:T(8,128)S(1)} %bitcast.6) | data formatting | bytes 1048576
  38.2 0.7 %copy.13 = f32[1,64,4,64]{3,2,1,0:T(4,128)} copy(f32[1,64,4,64]{3,2,1,0:T(4,128)S(1)} %bitcast.7) | data formatting | bytes 131072

commit v6 on v5

--- a/solution.py
+++ b/solution.py
@@ -446,11 +446,12 @@
         columns_there = slice(there * CORES * LANES, (there + 1) * CORES * LANES)
         block = times(weighted[...], spread[:, columns_there])
         back_out[there] = block.astype(jnp.bfloat16)
-        for mate in reversed(range(CORES)):
-
-            @pl.when(place != there * CORES + mate)
-            def send_back(there=there, mate=mate):
-                back_copy(there, mate).start()
+        if turn_of % 2:
+            for one, mate in ((there - 1, 1), (there, 1), (there - 1, 0), (there, 0)):
+
+                @pl.when(place != one * CORES + mate)
+                def send_back(one=one, mate=mate):
+                    back_copy(one, mate).start()
 
     back[place] = back_out[chip, :, lanes_of(core)]
 

time: 39 us -> 38.9 us (level); the launches traced: 38.9 us -> 38.2 us
  Pallas kernels: 36.2 us -> 35.5 us
    pallas_call x1, Pallas kernels: 36.2 us -> 35.5 us  [on_device(): pl.pallas_call(kernel, out_shape=(jax.ShapeDtypeStruct((nodes, width), jn...]
where the time goes in v6:
time: 38.9 us; the launch traced here: 38.2 us
  Pallas kernels  35.5 us (91%)
  local copies, waits for them, and re-layouts  1.45 us (4%)
  between operations  1.29 us (3%)
    pallas_call x1, Pallas kernels, on_device(): pl.pallas_call(kernel, out_shape=(jax.ShapeDtypeStruct((nodes, width), jn...  35.5 us
    unnamed x2, local copies, waits for them, and re-layouts  1.45 us

profile of v6, /device:TPU:1, one launch (start us, length us, event | category | flops | bytes accessed | tf_op | source)
XLA Modules:
  0.0 38.2 jit_solution(1234524655450140404)
XLA Ops:
  1.3 35.5 %shard_map.86 = (f32[64,2048]{1,0:T(8,128)S(1)}, f32[64,4,64]{2,1,0:T(4,128)S(1)}) custom-call(f32[64,2048]{1,0:T(8,128)} %bitcast.8, bf16[64,4,64]{2,1,0:T(4,128)(2,1)} %bitcast.9, f32[1,64]{1,0:T(1,128)} %bitcast.10, s32[1,64]{1,0:T(1,128)} %bitcast.11, s32[1]{0:T(128)S(6)} %copy.11.cluster, s32[1,2048]{1,0:T(1,128)} %mapping.1, s32[1,2048]{1,0:T(1,128)} %ranks.1), custom_call_target="tpu_custom_call" | custom-call | tf_op jit(solution)/shard_map/pallas_call | solution.py:512
  36.8 0.8 %copy.12 = f32[1,1,64,2048]{3,2,1,0:T(8,128)} copy(f32[1,1,64,2048]{3,2,1,0:T(8,128)S(1)} %bitcast.6) | data formatting | bytes 1048576
  37.6 0.7 %copy.13 = f32[1,64,4,64]{3,2,1,0:T(4,128)} copy(f32[1,64,4,64]{3,2,1,0:T(4,128)S(1)} %bitcast.7) | data formatting | bytes 131072

commit v7 on v6

--- a/solution.py
+++ b/solution.py
@@ -255,10 +255,15 @@
         target = far_peer(step)[-1]
         pl.semaphore_signal(barrier, inc=1, device_id=target, device_id_type=MESH)
 
-    for step in near_steps:
-        greet_near(step)
-    for step in far_steps:
-        greet_far(step)
+    around = [(min(step // CORES, chips - step // CORES), False, step) for step in far_steps]
+    across = [(hops(step), True, step) for step in near_steps]
+    merged = sorted(across + around, key=lambda item: -item[0])
+
+    for distance, in_plane, step in merged:
+        if in_plane:
+            greet_near(step)
+        else:
+            greet_far(step)
     for fetch in fetches[1:]:
         fetch.start()
 
@@ -291,10 +296,11 @@
     meta[slot] = meta_out[chunk]
     pl.semaphore_wait(barrier, HALVES * SLOTS - 1 + ring - 1)
 
-    for step in near_steps:
-        near_copy(step).start()
-    for step in far_steps:
-        cluster_copy(step).start()
+    for distance, in_plane, step in merged:
+        if in_plane:
+            near_copy(step).start()
+        else:
+            cluster_copy(step).start()
     each(SLOTS, lambda step: meta_copy(step).start())
 
     for fetch in fetches[3:5]:
@@ -463,20 +469,24 @@
         for index in range(CLUSTERS):
             held[index] = held[index] + jnp.where(theirs == index, block, 0.0)
     held = [part.reshape(SLOTS, CHUNK, LANES) for part in held]
-    for pair in range(CLUSTERS // 2):
-        rows = slice(pair * CHUNK, (pair + 1) * CHUNK)
-        first, second = held[2 * pair], held[2 * pair + 1]
-        last_out[:SLOTS, rows] = jnp.where(low, first, pltpu.roll(second, PIECE, 2))
-        last_out[SLOTS:, rows] = jnp.where(low, pltpu.roll(first, PIECE, 2), second)
-
     def lateness(there):
         return there // SLOTS * PLAYERS + there % PLAYERS + there % SLOTS // PLAYERS
 
-    for there in sorted(range(HALVES * SLOTS), key=lateness):
-
-        @pl.when(there != half * SLOTS + chunk)
-        def send_last(there=there):
-            last_copy(there).start()
+    for their_half in range(HALVES):
+        for pair in range(CLUSTERS // 2):
+            rows = slice(pair * CHUNK, (pair + 1) * CHUNK)
+            first, second = held[2 * pair], held[2 * pair + 1]
+            if their_half == 0:
+                piece = jnp.where(low, first, pltpu.roll(second, PIECE, 2))
+            else:
+                piece = jnp.where(low, pltpu.roll(first, PIECE, 2), second)
+            last_out[their_half * SLOTS : (their_half + 1) * SLOTS, rows] = piece
+        theirs = range(their_half * SLOTS, (their_half + 1) * SLOTS)
+        for there in sorted(theirs, key=lateness):
+
+            @pl.when(there != half * SLOTS + chunk)
+            def send_last(there=there):
+                last_copy(there).start()
 
     last[half * SLOTS + chunk] = last_out[half * SLOTS + slot]
 

time: 38.9 us -> 38.7 us (level)
  no operation moved by 1% of the time
where the time goes in v7:
time: 38.7 us; the launch traced here: 38 us
  Pallas kernels  35.2 us (91%)
  local copies, waits for them, and re-layouts  1.45 us (4%)
  between operations  1.29 us (3%)
    pallas_call x1, Pallas kernels, on_device(): pl.pallas_call(kernel, out_shape=(jax.ShapeDtypeStruct((nodes, width), jn...  35.2 us
    unnamed x2, local copies, waits for them, and re-layouts  1.45 us

profile of v7, /device:TPU:1, one launch (start us, length us, event | category | flops | bytes accessed | tf_op | source)
XLA Modules:
  0.0 38.0 jit_solution(5537685763462347212)
XLA Ops:
  1.3 35.2 %shard_map.86 = (f32[64,2048]{1,0:T(8,128)S(1)}, f32[64,4,64]{2,1,0:T(4,128)S(1)}) custom-call(f32[64,2048]{1,0:T(8,128)} %bitcast.8, bf16[64,4,64]{2,1,0:T(4,128)(2,1)} %bitcast.9, f32[1,64]{1,0:T(1,128)} %bitcast.10, s32[1,64]{1,0:T(1,128)} %bitcast.11, s32[1]{0:T(128)S(6)} %copy.11.cluster, s32[1,2048]{1,0:T(1,128)} %mapping.1, s32[1,2048]{1,0:T(1,128)} %ranks.1), custom_call_target="tpu_custom_call" | custom-call | tf_op jit(solution)/shard_map/pallas_call | solution.py:522
  36.5 0.8 %copy.12 = f32[1,1,64,2048]{3,2,1,0:T(8,128)} copy(f32[1,1,64,2048]{3,2,1,0:T(8,128)S(1)} %bitcast.6) | data formatting | bytes 1048576
  37.3 0.7 %copy.13 = f32[1,64,4,64]{3,2,1,0:T(4,128)} copy(f32[1,64,4,64]{3,2,1,0:T(4,128)S(1)} %bitcast.7) | data formatting | bytes 131072

commit v8 on v7

--- a/solution.py
+++ b/solution.py
@@ -316,9 +316,10 @@
             strength[lanes_of(block), span] = sign.astype(SMALL)
         return carry
 
-    lax.fori_loop(0, width // LANES, build_strength, 0)
-
+    lax.fori_loop(0, width // LANES // 2, build_strength, 0)
     each(SLOTS, lambda step: regret_copy(step).start())
+    lax.fori_loop(width // LANES // 2, width // LANES, build_strength, 0)
+
 
     await_bytes(near.at[pl.ds(1, HALVES * SLOTS - 1)], near_recv)
     await_bytes(clusters.at[pl.ds(1, ring - 1)], cluster_recv)

time: 38.7 us -> 38.7 us (level)
  no operation moved by 1% of the time
where the time goes in v8:
time: 38.7 us; the launch traced here: 37.9 us
  Pallas kernels  35.2 us (91%)
  local copies, waits for them, and re-layouts  1.45 us (4%)
  between operations  1.29 us (3%)
    pallas_call x1, Pallas kernels, on_device(): pl.pallas_call(kernel, out_shape=(jax.ShapeDtypeStruct((nodes, width), jn...  35.2 us
    unnamed x2, local copies, waits for them, and re-layouts  1.45 us

profile of v8, /device:TPU:1, one launch (start us, length us, event | category | flops | bytes accessed | tf_op | source)
XLA Modules:
  0.0 37.9 jit_solution(5569694722287690221)
XLA Ops:
  1.3 35.2 %shard_map.86 = (f32[64,2048]{1,0:T(8,128)S(1)}, f32[64,4,64]{2,1,0:T(4,128)S(1)}) custom-call(f32[64,2048]{1,0:T(8,128)} %bitcast.8, bf16[64,4,64]{2,1,0:T(4,128)(2,1)} %bitcast.9, f32[1,64]{1,0:T(1,128)} %bitcast.10, s32[1,64]{1,0:T(1,128)} %bitcast.11, s32[1]{0:T(128)S(6)} %copy.11.cluster, s32[1,2048]{1,0:T(1,128)} %mapping.1, s32[1,2048]{1,0:T(1,128)} %ranks.1), custom_call_target="tpu_custom_call" | custom-call | tf_op jit(solution)/shard_map/pallas_call | solution.py:523
  36.5 0.8 %copy.12 = f32[1,1,64,2048]{3,2,1,0:T(8,128)} copy(f32[1,1,64,2048]{3,2,1,0:T(8,128)S(1)} %bitcast.6) | data formatting | bytes 1048576
  37.3 0.7 %copy.13 = f32[1,64,4,64]{3,2,1,0:T(4,128)} copy(f32[1,64,4,64]{3,2,1,0:T(4,128)S(1)} %bitcast.7) | data formatting | bytes 131072
